TPU v7x, 256 devices: a whole 4x4x8 slice. The times are simulated.
256 devices in a mesh: seq: 32 (over y, x, core), head: 8 (over z).
Axes of the slice: x: 4, y: 4, z: 8, core: 2. Of those that a mesh axis runs over, the one named last changes fastest.
Arguments:
- query_rows: bfloat16 [8192, 1024], P('seq', 'head'), may hold values from -6 to 6
- key_rows: bfloat16 [8192, 1024], P('seq', 'head'), may hold values from -6 to 6
- value_rows: bfloat16 [8192, 2048], P('seq', 'head'), may hold values from -6 to 6
- output_gate: bfloat16 [8192, 2048], P('seq', 'head'), may hold values from -6 to 6
- write_rate: float32 [16, 8192], P('head', 'seq'), may hold values from 0.05 to 1
- log_decay: float32 [16, 8192], P('head', 'seq'), may hold values from -1.2 to 0, as said below
- out_weight: bfloat16 [2048, 2048], P(None, 'head'), may hold values from -0.125 to 0.125
- out_cotangent: bfloat16 [8192, 2048], P('seq', 'head'), may hold values from -6 to 6
- block_response: int32 [96], replicated, may hold values from 0 to 63, as said below
- prefix_owner: int32 [32], replicated, may hold values from 0 to 31, each once
Outputs:
- layer_out: bfloat16 [8192, 2048], P('seq', 'head')
- grad_query: float32 [8192, 1024], P('seq', 'head')
- grad_key: float32 [8192, 1024], P('seq', 'head')
- grad_value: float32 [8192, 2048], P('seq', 'head')
- grad_gate: float32 [8192, 2048], P('seq', 'head')
- grad_write: float32 [16, 8192], P('head', 'seq')
- grad_decay: float32 [16, 8192], P('head', 'seq')
- grad_weight: float32 [2048, 2048], P('seq', 'head')
Inputs may be any that keep to these rules, and one draw needn't show every extreme that they name: `block_response`: blocks of one response are consecutive and lie within the 3 blocks of one index of seq; responses appear in increasing order; each response has 1 to 3 blocks and one has exactly 3; every response of 0 to 63 appears. `prefix_owner`: each index of seq holds exactly one prompt's prefix. `log_decay`: every entry is negative.
All inputs are finite; a program needn't handle non-finite values.
Results may differ from a plain program's by a relative error of at most 0.015.
Values may be sent and summed in bfloat16 or wider, within the bound.
A program may use at most 64 MiB of HBM per device.

v0:
```python
from functools import partial

import jax
import jax.numpy as jnp
from jax import lax
from jax.sharding import PartitionSpec as P

DK = 128
DV = 128
SPAN = 64
PREFIX = 64
BLK_DEV = 3
RESP_PER = 2


highest = lax.Precision.HIGHEST
tiny_eps = 1e-06


def laid_out(parts, dim):
    parts = jnp.moveaxis(parts, 0, dim)
    lengths = parts.shape
    return parts.reshape(*lengths[:dim], lengths[dim] * lengths[dim + 1], *lengths[dim + 2 :])


def sent_to_all(x, axis):
    peers = lax.axis_size(axis)
    return lax.all_to_all(jnp.broadcast_to(x[None], (peers, *x.shape)), axis, 0, 0, tiled=True)


def gathered_copies(x, axis, dim):
    return laid_out(sent_to_all(x, axis), dim)


def in_blocks(x, dim, peers):
    before, after = (x.shape[:dim], x.shape[dim + 1 :])
    return jnp.moveaxis(x.reshape(*before, peers, -1, *after), dim, 0)


def summed_on_arrival(x, axis, dim):
    peers = lax.axis_size(axis)
    parts = lax.all_to_all(in_blocks(x, dim, peers), axis, 0, 0, tiled=True)
    return jnp.sum(parts.astype(jnp.float32), axis=0)


def unit_rows(raw_rows):
    return raw_rows * lax.rsqrt(jnp.sum(raw_rows * raw_rows, axis=-1, keepdims=True) + tiny_eps)


def span_parts(query_unit, key_unit, value_part, write_part, decay_part):
    span_len = decay_part.shape[-1]
    dim_key = key_unit.shape[-1]
    cumulative = jnp.cumsum(decay_part, axis=-1)
    row_ids = lax.broadcasted_iota(jnp.int32, (span_len, span_len), 0)
    col_ids = lax.broadcasted_iota(jnp.int32, (span_len, span_len), 1)
    strict = row_ids > col_ids
    causal = row_ids >= col_ids
    spread = cumulative[..., :, None] - cumulative[..., None, :]
    below_diag = jnp.where(strict, jnp.exp(jnp.where(strict, spread, 0.0)), 0.0)
    within = jnp.where(causal, jnp.exp(jnp.where(causal, spread, 0.0)), 0.0)
    key_key = jnp.einsum("...ik,...jk->...ij", key_unit, key_unit, precision=highest)
    system = jnp.eye(span_len, dtype=jnp.float32) + write_part[..., :, None] * below_diag * key_key
    growth = jnp.exp(cumulative)
    right_side = jnp.concatenate(
        [(write_part * growth)[..., None] * key_unit, write_part[..., None] * value_part], axis=-1
    )
    solved = lax.linalg.triangular_solve(
        system, right_side, left_side=True, lower=True, unit_diagonal=True
    )
    weights_w = solved[..., :dim_key]
    base_u = solved[..., dim_key:]
    query_key = jnp.einsum("...ik,...jk->...ij", query_unit, key_unit, precision=highest) * within
    remain = jnp.exp(cumulative[..., -1:] - cumulative)
    key_tail = remain[..., None] * key_unit
    transfer = growth[..., -1][..., None, None] * jnp.eye(dim_key, dtype=jnp.float32) - jnp.einsum(
        "...ck,...cl->...kl", weights_w, key_tail, precision=highest
    )
    offset = jnp.einsum("...cv,...ck->...vk", base_u, key_tail, precision=highest)
    return (transfer, offset, weights_w, base_u, query_key, growth, query_unit)


def span_apply(span_terms, state_in):
    transfer, offset, weights_w, base_u, query_key, growth, query_unit = span_terms
    update = base_u - jnp.einsum("...ck,...vk->...cv", weights_w, state_in, precision=highest)
    block_out = growth[..., None] * jnp.einsum(
        "...ck,...vk->...cv", query_unit, state_in, precision=highest
    )
    block_out = block_out + jnp.einsum("...ij,...jv->...iv", query_key, update, precision=highest)
    state_out = jnp.einsum("...vk,...kl->...vl", state_in, transfer, precision=highest) + offset
    return (block_out, state_out)


def split_heads(flat_rows, feat_width):
    return jnp.transpose(flat_rows.reshape(flat_rows.shape[0], -1, feat_width), (1, 0, 2))


def blocks_first(head_array):
    heads_count, row_total, feat_width = head_array.shape
    return jnp.transpose(
        head_array.reshape(heads_count, row_total // SPAN, SPAN, feat_width), (1, 0, 2, 3)
    )


def heads_first(block_array):
    block_total, heads_count, span_len, feat_width = block_array.shape
    return jnp.transpose(block_array, (1, 0, 2, 3)).reshape(
        heads_count, block_total * span_len, feat_width
    )


def region_inputs(query32, key32, value32, write_part, decay_part):
    heads_count = write_part.shape[0]
    query_unit = unit_rows(split_heads(query32, DK)) * DK ** (-0.5)
    key_unit = unit_rows(split_heads(key32, DK))
    repeat_by = heads_count // query_unit.shape[0]
    query_unit = jnp.repeat(query_unit, repeat_by, axis=0)
    key_unit = jnp.repeat(key_unit, repeat_by, axis=0)
    values = split_heads(value32, DV)
    return (
        blocks_first(query_unit),
        blocks_first(key_unit),
        blocks_first(values),
        blocks_first(write_part[..., None])[..., 0],
        blocks_first(decay_part[..., None])[..., 0],
    )


def prefix_pass(query32, key32, value32, write_part, decay_part):
    heads_count = write_part.shape[0]

    def prefix_advance(state_in, block_in):
        block_out, state_out = span_apply(span_parts(*block_in), state_in)
        return (state_out, block_out)

    last_state, block_outs = lax.scan(
        prefix_advance,
        jnp.zeros((heads_count, DV, DK), jnp.float32),
        region_inputs(query32, key32, value32, write_part, decay_part),
    )
    return (block_outs, last_state)


def answer_parts(query32, key32, value32, write_part, decay_part):
    return span_parts(*region_inputs(query32, key32, value32, write_part, decay_part))


def respond_blocks(span_terms, states_all, carry_in, block_flags, owners):

    def respond_advance(state_in, block_in):
        terms_here, block_flag, block_owner = block_in
        chosen = lax.dynamic_index_in_dim(states_all, block_owner, 0, keepdims=False)
        state_in = jnp.where(block_flag, chosen, state_in)
        block_out, state_out = span_apply(terms_here, state_in)
        return (state_out, block_out)

    ignored, block_outs = lax.scan(respond_advance, carry_in, (span_terms, block_flags, owners))
    return block_outs


def gated_norm(outs_all, gate32):
    inv_scale = lax.rsqrt(jnp.mean(outs_all * outs_all, axis=-1, keepdims=True) + tiny_eps)
    gated_rows = outs_all * inv_scale * jax.nn.silu(split_heads(gate32, DV))
    return jnp.transpose(gated_rows, (1, 0, 2)).reshape(gate32.shape[0], -1)


def per_device(
    query_rows,
    key_rows,
    value_rows,
    output_gate,
    write_rate,
    log_decay,
    out_weight,
    out_cotangent,
    block_response,
    prefix_owner,
):
    query32 = query_rows.astype(jnp.float32)
    key32 = key_rows.astype(jnp.float32)
    value32 = value_rows.astype(jnp.float32)
    gate32 = output_gate.astype(jnp.float32)
    heads_count = write_rate.shape[0]
    block_ids = lax.axis_index("seq") * BLK_DEV + jnp.arange(BLK_DEV, dtype=jnp.int32)
    current = jnp.take(block_response, block_ids)
    previous = jnp.take(block_response, jnp.maximum(block_ids - 1, 0))
    block_flags = (block_ids == 0) | (current != previous)
    owners = jnp.take(prefix_owner, current // RESP_PER)
    prefix_in = (
        query32[:PREFIX],
        key32[:PREFIX],
        value32[:PREFIX],
        write_rate[:, :PREFIX],
        log_decay[:, :PREFIX],
    )
    answer_in = (
        query32[PREFIX:],
        key32[PREFIX:],
        value32[PREFIX:],
        write_rate[:, PREFIX:],
        log_decay[:, PREFIX:],
    )
    (prefix_outs, prefix_last), prefix_pull = jax.vjp(prefix_pass, *prefix_in)
    shared = gathered_copies(prefix_last.astype(jnp.bfloat16)[None], "seq", 0)
    states_all = shared.astype(jnp.float32)
    span_terms, terms_pull = jax.vjp(answer_parts, *answer_in)
    zero_state = jnp.zeros((heads_count, DV, DK), jnp.float32)
    respond = partial(respond_blocks, carry_in=zero_state, block_flags=block_flags, owners=owners)
    answer_outs, answer_pull = jax.vjp(respond, span_terms, states_all)
    outs_all = jnp.concatenate([heads_first(prefix_outs), heads_first(answer_outs)], axis=1)
    normed, norm_pull = jax.vjp(gated_norm, outs_all, gate32)
    rounded = normed.astype(jnp.bfloat16)
    partial_out = jnp.einsum("rv,dv->rd", rounded, out_weight, preferred_element_type=jnp.float32)
    layer_out = lax.psum_scatter(partial_out, "head", scatter_dimension=1, tiled=True).astype(
        jnp.bfloat16
    )
    cotangent = gathered_copies(out_cotangent, "head", 1)
    grad_normed = jnp.dot(cotangent, out_weight, preferred_element_type=jnp.float32)
    grad_weight = summed_on_arrival(
        jnp.einsum("rd,rv->dv", cotangent, rounded, preferred_element_type=jnp.float32).astype(
            jnp.bfloat16
        ),
        "seq",
        0,
    )
    grad_outs, grad_gate = norm_pull(grad_normed)
    grad_prefix = blocks_first(grad_outs[:, :PREFIX])
    grad_answer = blocks_first(grad_outs[:, PREFIX:])
    grad_terms, grad_states = answer_pull(grad_answer)
    pieces = lax.all_to_all(
        grad_states.astype(jnp.bfloat16), "seq", split_axis=0, concat_axis=0, tiled=True
    ).astype(grad_states.dtype)
    own_state = jnp.sum(pieces, axis=0)
    prefix_grads = prefix_pull((grad_prefix, own_state))
    answer_grads = terms_pull(grad_terms)
    grad_query = jnp.concatenate([prefix_grads[0], answer_grads[0]], axis=0)
    grad_key = jnp.concatenate([prefix_grads[1], answer_grads[1]], axis=0)
    grad_value = jnp.concatenate([prefix_grads[2], answer_grads[2]], axis=0)
    grad_write = jnp.concatenate([prefix_grads[3], answer_grads[3]], axis=1)
    grad_decay = jnp.concatenate([prefix_grads[4], answer_grads[4]], axis=1)
    return (
        layer_out,
        grad_query,
        grad_key,
        grad_value,
        grad_gate,
        grad_write,
        grad_decay,
        grad_weight,
    )


def solution(mesh):
    placed = (
        P("seq", "head"),
        P("seq", "head"),
        P("seq", "head"),
        P("seq", "head"),
        P("head", "seq"),
        P("head", "seq"),
        P(None, "head"),
        P("seq", "head"),
        P(),
        P(),
    )
    return jax.shard_map(
        per_device,
        mesh=mesh,
        in_specs=placed,
        out_specs=(
            P("seq", "head"),
            P("seq", "head"),
            P("seq", "head"),
            P("seq", "head"),
            P("seq", "head"),
            P("head", "seq"),
            P("head", "seq"),
            P("seq", "head"),
        ),
        check_vma=False,
    )
```

profile of v0, /device:TPU:1, one launch (start us, length us, event | category | flops | bytes accessed | tf_op | source)
XLA Modules:
  0.0 294.9 jit_solution(6103577155595876104)
XLA Ops:
  7.2 2.0 broadcast_in_dim.440
  9.2 9.1 %all-to-all-start.1 = ((bf16[8,256,256]{2,1,0:T(8,128)(2,1)}), bf16[8,256,256]{2,1,0:T(8,128)(2,1)S(1)}, u32[]{:S(2)}, u32[]{:S(2)}) async-start(bf16[8,256,256]{2,1,0:T(8,128)(2,1)} %broadcast_in_dim.440), calls=%async_computation.2 | async-start | bytes 2097152 | tf_op jit(solution)/shard_map/all_to_all | solution.py:28
  33.6 1.3 gather_fusion.2
  35.8 9.8 %custom-call.22 = f32[2,1,64,64]{2,3,1,0:T(8,128)S(1)} custom-call(f32[2,1,64,64]{3,2,1,0:T(8,128)S(1)} %fusion.188), custom_call_target="InvertDiagBlocksLowerTriangular" | custom-call | tf_op jit(solution)/shard_map/jvp()/while/body/eval_jaxpr/triangular_solve | solution.py:67
  47.6 30.9 %custom-call.23 = f32[3,2,1,64,64]{3,4,2,1,0:T(8,128)} custom-call(f32[3,2,1,64,64]{4,3,2,1,0:T(8,128)} %get-tuple-element.1479), custom_call_target="InvertDiagBlocksLowerTriangular" | custom-call | tf_op jit(solution)/shard_map/jvp()/triangular_solve | solution.py:67
  78.5 1.4 copy.260
  84.9 1.9 broadcast_in_dim.432
  86.7 8.2 %all-to-all-start = ((bf16[32,1,2,128,128]{4,3,2,1,0:T(8,128)(2,1)}), bf16[32,1,2,128,128]{4,3,2,1,0:T(8,128)(2,1)}, u32[]{:S(2)}, u32[]{:S(2)}) async-start(bf16[32,1,2,128,128]{4,3,2,1,0:T(8,128)(2,1)} %broadcast_in_dim.432), calls=%async_computation | async-start | bytes 4194304 | tf_op jit(solution)/shard_map/all_to_all | solution.py:28
  99.7 1.6 copy.191
  101.3 2.4 reshape.768
  104.8 18.0 %all-to-all-done = bf16[32,1,2,128,128]{4,3,2,1,0:T(8,128)(2,1)} async-done(((bf16[32,1,2,128,128]{4,3,2,1,0:T(8,128)(2,1)}), bf16[32,1,2,128,128]{4,3,2,1,0:T(8,128)(2,1)}, u32[]{:S(2)}, u32[]{:S(2)}) %all-to-all-start) | async-done | bytes 2097184 | tf_op jit(solution)/shard_map/all_to_all | solution.py:28
  122.8 4.0 %bitcast_convert_fusion = f32[32,2,128,128]{3,2,1,0:T(8,128)} fusion(bf16[32,1,2,128,128]{4,3,2,1,0:T(8,128)(2,1)} %all-to-all-done), kind=kLoop, calls=%fused_computation.96 | loop fusion | flops 1048576 | bytes 6291456 | tf_op jit(solution)/shard_map/convert_element_type | solution.py:204
  127.7 22.6 %while.17 = (s32[]{:T(128)}, f32[2,128,128]{2,1,0:T(8,128)S(1)}, f32[3,2,64,128]{3,2,1,0:T(8,128)}, s32[3]{0:T(128)S(1)}, f32[3,2,128,128]{3,2,1,0:T(8,128)S(1)}...) while((s32[]{:T(128)}, f32[2,128,128]{2,1,0:T(8,128)S(1)}, ...), condition=%wide.region_7.9_spmd.clone.clone, body=%wide.region_6.8_spmd.clone.sunk.clone | while | flops 113393664 | bytes 2040072 | solution.py:156
  130.9 1.6 bitcast_dynamic-update-slice_fusion.15
  138.4 1.6 bitcast_dynamic-update-slice_fusion.15
  146.0 1.6 bitcast_dynamic-update-slice_fusion.15
  151.7 2.2 multiply_reduce_fusion.1
  158.4 2.4 broadcast_in_dim.443
  160.8 31.1 %while.18 = (s32[]{:T(128)}, f32[32,2,128,128]{2,3,1,0:T(8,128)}, f32[2,128,128]{1,2,0:T(8,128)S(1)}, f32[3,2,128,128]{3,2,1,0:T(8,128)S(1)}, f32[3,2,128,128]{2...) while((s32[]{:T(128)}, f32[32,2,128,128]{2,3,1,0:T(8,128)}, ...), condition=%wide.region_15.17_spmd.clone.clone, body=%wide.region_13.16_spmd.clone.sunk.clone | while | flops 226852736 | bytes 3488007 | solution.py:156
  167.3 3.2 %fusion.401 = (f32[32,2,128,128]{2,3,1,0:T(8,128)}, f32[2,128,128]{1,2,0:T(8,128)S(1)}) fusion(f32[32,2,128,128]{2,3,1,0:T(8,128)} %get-tuple-element.1937, s32[]{:T(128)} %bitcast.435, pred[]{:T(512)} %bitcast.436, f32[2,128,128]{1,2,0:T(8,128)S(1)} %convolution_add_fusion.25, f32[3,2,64,128]{3,2,1,0:T(8,128)S(1)} %get-tuple-element.1974, ...), kind=kOutput, calls=%fused_computation.44.clone.1.clone | convolution fusion | flops 25280512 | bytes 656388 | tf_op jit(solution)/shard_map/transpose(jvp())/while/body/eval_jaxpr/...ck,...vk->...cv/dot_general | solution.py:84
  177.6 3.2 %fusion.401 = (f32[32,2,128,128]{2,3,1,0:T(8,128)}, f32[2,128,128]{1,2,0:T(8,128)S(1)}) fusion(f32[32,2,128,128]{2,3,1,0:T(8,128)} %get-tuple-element.1937, s32[]{:T(128)} %bitcast.435, pred[]{:T(512)} %bitcast.436, f32[2,128,128]{1,2,0:T(8,128)S(1)} %convolution_add_fusion.25, f32[3,2,64,128]{3,2,1,0:T(8,128)S(1)} %get-tuple-element.1974, ...), kind=kOutput, calls=%fused_computation.44.clone.1.clone | convolution fusion | flops 25280512 | bytes 656388 | tf_op jit(solution)/shard_map/transpose(jvp())/while/body/eval_jaxpr/...ck,...vk->...cv/dot_general | solution.py:84
  187.9 3.2 %fusion.401 = (f32[32,2,128,128]{2,3,1,0:T(8,128)}, f32[2,128,128]{1,2,0:T(8,128)S(1)}) fusion(f32[32,2,128,128]{2,3,1,0:T(8,128)} %get-tuple-element.1937, s32[]{:T(128)} %bitcast.435, pred[]{:T(512)} %bitcast.436, f32[2,128,128]{1,2,0:T(8,128)S(1)} %convolution_add_fusion.25, f32[3,2,64,128]{3,2,1,0:T(8,128)S(1)} %get-tuple-element.1974, ...), kind=kOutput, calls=%fused_computation.44.clone.1.clone | convolution fusion | flops 25280512 | bytes 656388 | tf_op jit(solution)/shard_map/transpose(jvp())/while/body/eval_jaxpr/...ck,...vk->...cv/dot_general | solution.py:84
  192.7 1.8 convolution_add_fusion.6
  194.5 1.5 fusion.301
  196.0 1.4 convolution_add_fusion.7
  198.7 1.4 fusion.88
  202.1 1.8 fusion.309
  203.9 1.7 fusion.66
  205.7 1.4 copy.229
  207.1 6.2 %all-to-all-start.3 = ((bf16[32,64,256]{2,1,0:T(8,128)(2,1)}), bf16[32,64,256]{2,1,0:T(8,128)(2,1)S(1)}, u32[]{:S(2)}, u32[]{:S(2)}) async-start(bf16[32,64,256]{2,1,0:T(8,128)(2,1)} %bitcast.453), calls=%async_computation.4 | async-start | bytes 2097152 | tf_op jit(solution)/shard_map/all_to_all | solution.py:42
  214.0 1.4 convolution_add_fusion.9
  216.4 1.5 fusion.68
  217.9 1.3 fusion.69
  219.3 1.8 fusion.108
  221.5 3.9 %convert_element_type.96 = bf16[32,2,128,128]{2,3,1,0:T(8,128)(2,1)} convert(f32[32,2,128,128]{2,3,1,0:T(8,128)} %get-tuple-element.1130) | non-fusion elementwise | flops 1048576 | bytes 6291456 | tf_op jit(solution)/shard_map/convert_element_type | solution.py:230
  228.6 2.0 all-to-all-done.3
  230.6 5.5 %all-to-all-start.2 = ((bf16[32,2,128,128]{2,3,1,0:T(8,128)(2,1)}), bf16[32,2,128,128]{2,3,1,0:T(8,128)(2,1)S(1)}, u32[]{:S(2)}, u32[]{:S(2)}) async-start(bf16[32,2,128,128]{2,3,1,0:T(8,128)(2,1)} %convert_element_type.96), calls=%async_computation.3 | async-start | bytes 4194304 | tf_op jit(solution)/shard_map/all_to_all | solution.py:229
  236.1 1.6 multiply_reduce_fusion.10
  239.1 3.3 %reduce_window_sum.56 = f32[3,2,64,1]{3,2,1,0:T(8,128)} reduce-window(f32[3,2,64,1]{3,2,1,0:T(8,128)} %copy.227, f32[]{:T(128)} %constant.325.clone.1), window={size=1x1x64x1 pad=0_0x0_0x0_63x0_0}, to_apply=%region_41.43 | reduce-window | flops 24192 | bytes 3076 | tf_op jit(solution)/shard_map/transpose(jvp(jit(cumsum)))/reduce_window_sum | solution.py:53
  249.2 1.2 fusion.217
  251.8 1.7 fusion.199
  253.6 1.7 add_add_fusion.1
  255.2 1.7 add_add_fusion.2
  257.7 6.2 %all-to-all-done.2 = bf16[32,2,128,128]{2,3,1,0:T(8,128)(2,1)S(1)} async-done(((bf16[32,2,128,128]{2,3,1,0:T(8,128)(2,1)}), bf16[32,2,128,128]{2,3,1,0:T(8,128)(2,1)S(1)}, u32[]{:S(2)}, u32[]{:S(2)}) %all-to-all-start.2) | async-done | bytes 2097184 | tf_op jit(solution)/shard_map/all_to_all | solution.py:229
  265.8 1.2 convolution_add_fusion.14
  276.2 1.3 pad_maximum_fusion.5
  277.5 1.3 pad_maximum_fusion.4
  286.5 1.6 convert_element_type.95
  (389 shorter events, 106.0 us)
Async XLA Ops:
  7.2 17.3 %copy-start = (s32[96]{0:T(128)S(1)}, s32[96]{0:T(128)}, u32[]{:S(2)}) copy-start(s32[96]{0:T(128)} %param.24) | copy-start | bytes 1156
  7.2 19.2 %copy-start.71 = (f32[2,256]{1,0:T(2,128)S(1)}, f32[2,256]{1,0:T(2,128)}, u32[]{:S(2)}) copy-start(f32[2,256]{1,0:T(2,128)} %param.20) | copy-start | bytes 6148
  7.2 18.0 %copy-start.1 = (s32[32]{0:T(128)S(1)}, s32[32]{0:T(128)}, u32[]{:S(2)}) copy-start(s32[32]{0:T(128)} %param.25) | copy-start | bytes 388
  7.2 25.0 %copy-start.22 = (bf16[256,256]{1,0:T(8,128)(2,1)S(1)}, bf16[256,256]{1,0:T(8,128)(2,1)}, u32[]{:S(2)}) copy-start(bf16[256,256]{1,0:T(8,128)(2,1)} %param.18) | copy-start | bytes 393220
  9.2 36.4 %copy-start.52 = (bf16[256,256]{1,0:T(8,128)(2,1)S(1)}, bf16[256,256]{1,0:T(8,128)(2,1)}, u32[]{:S(2)}) copy-start(bf16[256,256]{1,0:T(8,128)(2,1)} %param.19) | copy-start | bytes 393220
  9.2 69.3 %copy-start.2 = (bf16[2048,256]{1,0:T(8,128)(2,1)S(1)}, bf16[2048,256]{1,0:T(8,128)(2,1)}, u32[]{:S(2)}) copy-start(bf16[2048,256]{1,0:T(8,128)(2,1)} %param.22) | copy-start | bytes 3145732
  9.2 75.6 %all-to-all-start.1 = ((bf16[8,256,256]{2,1,0:T(8,128)(2,1)}), bf16[8,256,256]{2,1,0:T(8,128)(2,1)S(1)}, u32[]{:S(2)}, u32[]{:S(2)}) async-start(bf16[8,256,256]{2,1,0:T(8,128)(2,1)} %broadcast_in_dim.440), calls=%async_computation.2 | async-start | bytes 2097152 | tf_op jit(solution)/shard_map/all_to_all | solution.py:28
  19.8 78.9 %copy-start.13 = (f32[128,128]{1,0:T(8,128)}, f32[128,128]{1,0:T(8,128)S(1)}, u32[]{:S(2)}) copy-start(f32[128,128]{1,0:T(8,128)S(1)} %fusion.210) | copy-start | bytes 196612
  20.7 59.3 %copy-start.4 = (f32[256,128]{1,0:T(8,128)}, f32[256,128]{1,0:T(8,128)S(1)}, u32[]{:S(2)}) copy-start(f32[256,128]{1,0:T(8,128)S(1)} %convert_element_type.84) | copy-start | bytes 393220
  21.8 60.2 %copy-start.6 = (f32[256,128]{1,0:T(8,128)}, f32[256,128]{1,0:T(8,128)S(1)}, u32[]{:S(2)}) copy-start(f32[256,128]{1,0:T(8,128)S(1)} %convert_element_type.85) | copy-start | bytes 393220
  22.3 57.6 %copy-start.41 = (f32[2,64]{1,0:T(2,128)}, f32[2,64]{1,0:T(2,128)S(1)}, u32[]{:S(2)}) copy-start(f32[2,64]{1,0:T(2,128)S(1)} %reduce_window_sum.52) | copy-start | bytes 1540
  23.5 56.5 %copy-start.58 = (f32[2,3,64,1]{2,1,0,3:T(4,128)}, f32[2,3,64,1]{2,1,0,3:T(4,128)S(1)}, u32[]{:S(2)}) copy-start(f32[2,3,64,1]{2,1,0,3:T(4,128)S(1)} %broadcast_in_dim.434) | copy-start | bytes 4612
  23.5 56.5 %copy-start.55 = (f32[2,3,64,1]{2,0,1,3:T(2,128)}, f32[2,3,64,1]{2,0,1,3:T(2,128)S(1)}, u32[]{:S(2)}) copy-start(f32[2,3,64,1]{2,0,1,3:T(2,128)S(1)} %copy.330) | copy-start | bytes 4612
  28.2 51.8 %copy-start.53 = (f32[3,2,64]{2,1,0:T(2,128)}, f32[3,2,64]{2,1,0:T(2,128)S(1)}, u32[]{:S(2)}) copy-start(f32[3,2,64]{2,1,0:T(2,128)S(1)} %get-tuple-element.1874) | copy-start | bytes 4612
  28.3 51.7 %copy-start.44 = (pred[64,64]{1,0:T(8,128)(4,1)}, pred[64,64]{1,0:T(8,128)(4,1)S(1)}, u32[]{:S(2)}) copy-start(pred[64,64]{1,0:T(8,128)(4,1)S(1)} %get-tuple-element.1503) | copy-start | bytes 12292
  28.3 51.7 %copy-start.50 = (pred[64,64]{1,0:T(8,128)(4,1)}, pred[64,64]{1,0:T(8,128)(4,1)S(1)}, u32[]{:S(2)}) copy-start(pred[64,64]{1,0:T(8,128)(4,1)S(1)} %get-tuple-element.1504) | copy-start | bytes 12292
  28.9 97.9 %copy-start.16 = (f32[192,128]{1,0:T(8,128)}, f32[192,128]{1,0:T(8,128)S(1)}, u32[]{:S(2)}) copy-start(f32[192,128]{1,0:T(8,128)S(1)} %multiply_multiply_fusion) | copy-start | bytes 294916
  45.7 41.1 %copy-start.30 = (f32[2,1,64,64]{2,3,1,0:T(8,128)}, f32[2,1,64,64]{2,3,1,0:T(8,128)S(1)}, u32[]{:S(2)}) copy-start(f32[2,1,64,64]{2,3,1,0:T(8,128)S(1)} %custom-call.22) | copy-start | bytes 98308
  47.6 48.8 %copy-start.11 = (f32[192,2,128]{2,1,0:T(2,128)}, f32[192,2,128]{2,1,0:T(2,128)S(1)}, u32[]{:S(2)}) copy-start(f32[192,2,128]{2,1,0:T(2,128)S(1)} %reshape.722) | copy-start | bytes 589828
  80.0 15.0 %copy-start.73 = (s32[3]{0:T(128)S(1)}, s32[3]{0:T(128)}, u32[]{:S(2)}) copy-start(s32[3]{0:T(128)} %copy-done.72) | copy-start | bytes 40
  80.0 15.0 %copy-start.76 = (s32[3]{0:T(128)S(1)}, s32[3]{0:T(128)}, u32[]{:S(2)}) copy-start(s32[3]{0:T(128)} %gather_fusion.2) | copy-start | bytes 40
  80.0 15.4 %copy-start.65 = (f32[2,64]{1,0:T(2,128)S(1)}, f32[2,64]{1,0:T(2,128)}, u32[]{:S(2)}) copy-start(f32[2,64]{1,0:T(2,128)} %copy-done.64) | copy-start | bytes 1540
  80.1 16.3 %copy-start.61 = (f32[3,2,64]{2,1,0:T(2,128)}, f32[3,2,64]{2,1,0:T(2,128)S(1)}, u32[]{:S(2)}) copy-start(f32[3,2,64]{2,1,0:T(2,128)S(1)} %fusion.277) | copy-start | bytes 4612
  80.1 15.4 %copy-start.42 = (f32[2,64]{1,0:T(2,128)S(1)}, f32[2,64]{1,0:T(2,128)}, u32[]{:S(2)}) copy-start(f32[2,64]{1,0:T(2,128)} %copy-done.41) | copy-start | bytes 1540
  80.8 15.6 %copy-start.36 = (f32[64,128]{1,0:T(8,128)}, f32[64,128]{1,0:T(8,128)S(1)}, u32[]{:S(2)}) copy-start(f32[64,128]{1,0:T(8,128)S(1)} %multiply_multiply_fusion.1) | copy-start | bytes 98308
  80.8 15.6 %copy-start.56 = (f32[2,3,64,1]{2,0,1,3:T(2,128)S(1)}, f32[2,3,64,1]{2,0,1,3:T(2,128)}, u32[]{:S(2)}) copy-start(f32[2,3,64,1]{2,0,1,3:T(2,128)} %copy-done.55) | copy-start | bytes 4612
  81.0 15.6 %copy-start.33 = (f32[2,64,128]{2,1,0:T(8,128)}, f32[2,64,128]{2,1,0:T(8,128)S(1)}, u32[]{:S(2)}) copy-start(f32[2,64,128]{2,1,0:T(8,128)S(1)} %fusion.208) | copy-start | bytes 196612
  86.7 36.0 %all-to-all-start = ((bf16[32,1,2,128,128]{4,3,2,1,0:T(8,128)(2,1)}), bf16[32,1,2,128,128]{4,3,2,1,0:T(8,128)(2,1)}, u32[]{:S(2)}, u32[]{:S(2)}) async-start(bf16[32,1,2,128,128]{4,3,2,1,0:T(8,128)(2,1)} %broadcast_in_dim.432), calls=%async_computation | async-start | bytes 4194304 | tf_op jit(solution)/shard_map/all_to_all | solution.py:28
  104.8 22.8 %copy-start.54 = (f32[3,2,64]{2,1,0:T(2,128)S(1)}, f32[3,2,64]{2,1,0:T(2,128)}, u32[]{:S(2)}) copy-start(f32[3,2,64]{2,1,0:T(2,128)} %copy-done.53) | copy-start | bytes 4612
  104.8 22.8 %copy-start.68 = (f32[3,2,64,1]{2,1,3,0:T(2,128)S(1)}, f32[3,2,64,1]{2,1,3,0:T(2,128)}, u32[]{:S(2)}) copy-start(f32[3,2,64,1]{2,1,3,0:T(2,128)} %custom-call.32) | copy-start | bytes 4612
  104.8 22.8 %copy-start.80 = (s32[3]{0:T(128)S(1)}, s32[3]{0:T(128)}, u32[]{:S(2)}) copy-start(s32[3]{0:T(128)} %and_select_fusion.1) | copy-start | bytes 40
  104.8 22.8 %copy-start.81 = (s32[3]{0:T(128)S(1)}, s32[3]{0:T(128)}, u32[]{:S(2)}) copy-start(s32[3]{0:T(128)} %custom-call.33) | copy-start | bytes 40
  127.6 24.1 %copy-start.18 = (f32[256,2,128]{2,0,1:T(8,128)S(1)}, f32[256,2,128]{2,0,1:T(8,128)}, u32[]{:S(2)}) copy-start(f32[256,2,128]{2,0,1:T(8,128)} %copy.189) | copy-start | bytes 786436
  127.6 24.1 %copy-start.47 = (f32[2,64,128]{2,1,0:T(8,128)S(1)}, f32[2,64,128]{2,1,0:T(8,128)}, u32[]{:S(2)}) copy-start(f32[2,64,128]{2,1,0:T(8,128)} %convolution_add_fusion.19) | copy-start | bytes 196612
  160.8 31.1 %copy-start.14 = (f32[128,128]{1,0:T(8,128)S(1)}, f32[128,128]{1,0:T(8,128)}, u32[]{:S(2)}) copy-start(f32[128,128]{1,0:T(8,128)} %copy-done.13) | copy-start | bytes 196612
  207.1 23.5 %all-to-all-start.3 = ((bf16[32,64,256]{2,1,0:T(8,128)(2,1)}), bf16[32,64,256]{2,1,0:T(8,128)(2,1)S(1)}, u32[]{:S(2)}, u32[]{:S(2)}) async-start(bf16[32,64,256]{2,1,0:T(8,128)(2,1)} %bitcast.453), calls=%async_computation.4 | async-start | bytes 2097152 | tf_op jit(solution)/shard_map/all_to_all | solution.py:42
  213.3 73.2 %reduce-scatter.2.cloned.1.call-start = ((), (), s32[]{:S(2)}) async-start(), calls=%async_computation.5 | async-start | bytes 2359296 | tf_op jit(solution)/shard_map/reduce_scatter | solution.py:213
  225.4 20.3 %copy-start.7 = (f32[256,128]{1,0:T(8,128)S(1)}, f32[256,128]{1,0:T(8,128)}, u32[]{:S(2)}) copy-start(f32[256,128]{1,0:T(8,128)} %copy-done.6) | copy-start | bytes 393220
  225.4 21.4 %copy-start.5 = (f32[256,128]{1,0:T(8,128)S(1)}, f32[256,128]{1,0:T(8,128)}, u32[]{:S(2)}) copy-start(f32[256,128]{1,0:T(8,128)} %copy-done.4) | copy-start | bytes 393220
  230.6 33.2 %all-to-all-start.2 = ((bf16[32,2,128,128]{2,3,1,0:T(8,128)(2,1)}), bf16[32,2,128,128]{2,3,1,0:T(8,128)(2,1)S(1)}, u32[]{:S(2)}, u32[]{:S(2)}) async-start(bf16[32,2,128,128]{2,3,1,0:T(8,128)(2,1)} %convert_element_type.96), calls=%async_computation.3 | async-start | bytes 4194304 | tf_op jit(solution)/shard_map/all_to_all | solution.py:229
  236.1 29.3 %copy-start.15 = (f32[128,128]{1,0:T(8,128)S(1)}, f32[128,128]{1,0:T(8,128)}, u32[]{:S(2)}) copy-start(f32[128,128]{1,0:T(8,128)} %copy-done.13) | copy-start | bytes 196612
  244.1 29.5 %copy-start.43 = (f32[2,64]{1,0:T(2,128)S(1)}, f32[2,64]{1,0:T(2,128)}, u32[]{:S(2)}) copy-start(f32[2,64]{1,0:T(2,128)} %copy-done.41) | copy-start | bytes 1540
  245.8 33.0 %copy-start.37 = (f32[64,128]{1,0:T(8,128)S(1)}, f32[64,128]{1,0:T(8,128)}, u32[]{:S(2)}) copy-start(f32[64,128]{1,0:T(8,128)} %copy-done.36) | copy-start | bytes 98308
  257.7 15.0 %copy-start.31 = (f32[2,1,64,64]{2,3,1,0:T(8,128)S(1)}, f32[2,1,64,64]{2,3,1,0:T(8,128)}, u32[]{:S(2)}) copy-start(f32[2,1,64,64]{2,3,1,0:T(8,128)} %copy-done.30) | copy-start | bytes 98308
  257.7 27.4 %copy-start.39 = (f32[192,128]{1,0:T(8,128)S(1)}, f32[192,128]{1,0:T(8,128)}, u32[]{:S(2)}) copy-start(f32[192,128]{1,0:T(8,128)} %add_add_fusion.2) | copy-start | bytes 294916
  257.7 28.1 %copy-start.27 = (f32[2,24,8,128]{3,2,0,1:T(8,128)S(1)}, f32[2,24,8,128]{3,2,0,1:T(8,128)}, u32[]{:S(2)}) copy-start(f32[2,24,8,128]{3,2,0,1:T(8,128)} %copy.327) | copy-start | bytes 589828
  264.1 17.8 %copy-start.46 = (f32[2,64,128]{2,1,0:T(8,128)S(1)}, f32[2,64,128]{2,1,0:T(8,128)}, u32[]{:S(2)}) copy-start(f32[2,64,128]{2,1,0:T(8,128)} %fusion.199) | copy-start | bytes 196612
  264.1 19.6 %copy-start.40 = (f32[192,128]{1,0:T(8,128)S(1)}, f32[192,128]{1,0:T(8,128)}, u32[]{:S(2)}) copy-start(f32[192,128]{1,0:T(8,128)} %add_add_fusion.1) | copy-start | bytes 294916
  (39 other events, 315.1 us)
Sparse Core Ops, SparseCore 0:
  216.7 39.6 reduce-scatter.1
where the time goes:
time: 299 us; the launch traced here: 295 us
  other arithmetic  94 us (31%)
  matrix products  75.5 us (25%)
  local copies, waits for them, and re-layouts  47.7 us (16%)
  starting transfers between devices  29.1 us (10%)
  waiting for transfers between devices  26.8 us (9%)
  between operations  15.5 us (5%)
  loops' own time  6.3 us (2%)
    another operation x4, other arithmetic, span_parts(): lax.linalg.triangular_solve(system, right_side, left_side=True, lower=Tru...  40.8 us
    all_to_all x2, waiting for transfers between devices, sent_to_all(): lax.all_to_all(jnp.broadcast_to(x[None], (peers, *x.shape)), axis, 0, 0,...  18 us
    all_to_all x2, starting transfers between devices, sent_to_all(): lax.all_to_all(jnp.broadcast_to(x[None], (peers, *x.shape)), axis, 0, 0,...  17.4 us
    dot_general x11, matrix products, span_apply(): jnp.einsum('...ck,...vk->...cv', weights_w, state_in, precision=highest)  16.7 us
    dot_general x12, matrix products, span_apply(): jnp.einsum('...ij,...jv->...iv', query_key, update, precision=highest)  11.1 us
    dot_general x6, matrix products, span_parts(): jnp.einsum('...ck,...cl->...kl', weights_w, key_tail, precision=highest)  7.61 us
    dot_general x6, matrix products, span_parts(): jnp.einsum('...cv,...ck->...vk', base_u, key_tail, precision=highest)  7.26 us
    dynamic_slice x12, local copies, waits for them, and re-layouts, respond_blocks(): lax.scan(respond_advance, carry_in, (span_terms, block_flags, owners))  7.03 us
  transfers between devices with their start and end apart: 5, of which 3 were waited for; matrix products, arithmetic and copies ran while one was open for 45% of the time, Pallas kernels for 0%

commit v1 on v0

v1 whole, which is shorter than its diff:
```python
import functools

import jax
import jax.numpy as jnp
from jax import lax
from jax.experimental import pallas as pl
from jax.experimental.pallas import tpu as pltpu
from jax.sharding import PartitionSpec as P

N_SEQ = 32
N_HEAD = 8
CHIPS = 16
SPAN = 64
EPS = 1e-06
F32 = jnp.float32
BF16 = jnp.bfloat16
HIGHEST = lax.Precision.HIGHEST
MESH = pl.DeviceIdType.MESH
SCALE = 128 ** (-0.5)

KINDS = {"nn": ((1,), (0,)), "nt": ((1,), (1,)), "tn": ((0,), (0,))}


def dot(a, b, kind="nn"):
    return lax.dot_general(
        a.astype(BF16), b.astype(BF16), (KINDS[kind], ((), ())), preferred_element_type=F32
    )


def parts(x):
    high = x.astype(BF16)
    return high, (x - high.astype(F32)).astype(BF16)


def dot3(a, b, kind="nn"):
    a_high, a_low = parts(a)
    b_high, b_low = parts(b)
    return dot(a_high, b_high, kind) + (dot(a_high, b_low, kind) + dot(a_low, b_high, kind))


def dot_exact(a, b):
    return lax.dot_general(
        a, b, (KINDS["nn"], ((), ())), precision=HIGHEST, preferred_element_type=F32
    )


def iotas(shape=(128, 128)):
    return lax.broadcasted_iota(jnp.int32, shape, 0), lax.broadcasted_iota(jnp.int32, shape, 1)


def stack_heads(x):
    return jnp.concatenate([x[:, :128], x[:, 128:]], axis=0)


def side_heads(x):
    return jnp.concatenate([x[:64], x[64:]], axis=1)


def diagonal_heads(x):
    zero = jnp.zeros_like(x[:64])
    return jnp.concatenate(
        [jnp.concatenate([x[:64], zero], axis=1), jnp.concatenate([zero, x[64:]], axis=1)], axis=0
    )


def twice(x):
    return jnp.concatenate([x, x], axis=0)


def fold(x):
    return x[:64] + x[64:]


def half_swap(x):
    return jnp.concatenate([x[:, 64:], x[:, :64]], axis=1)


def by_block(x):
    lower = lax.broadcasted_iota(jnp.int32, (1, 128), 1) < 64
    rows = []
    for pair in range(2):
        first = x[0:1, 128 * pair : 128 * pair + 128]
        second = x[1:2, 128 * pair : 128 * pair + 128]
        rows.append(jnp.where(lower, first, half_swap(second)))
        rows.append(jnp.where(lower, half_swap(first), second))
    return jnp.concatenate(rows, axis=0)


def by_head(x):
    lower = lax.broadcasted_iota(jnp.int32, (1, 128), 1) < 64
    heads = ([], [])
    for pair in range(2):
        even, odd = x[2 * pair : 2 * pair + 1], x[2 * pair + 1 : 2 * pair + 2]
        heads[0].append(jnp.where(lower, even, half_swap(odd)))
        heads[1].append(jnp.where(lower, half_swap(even), odd))
    return jnp.concatenate([jnp.concatenate(row, axis=1) for row in heads], axis=0)


def turned(x):
    return jnp.transpose(jnp.concatenate([x, jnp.zeros((120, 128), F32)], axis=0))


def unit_scale(x):
    return lax.rsqrt(jnp.sum(x * x, axis=-1, keepdims=True) + EPS)


def running_decay(write_rate, log_decay):
    row, col = iotas()
    same = (row >> 6) == (col >> 6)
    upto = jnp.where(same & (row <= col), 1.0, 0.0).astype(F32)
    both = jnp.concatenate([by_block(log_decay), by_block(write_rate)], axis=0)
    summed = dot_exact(both, upto)
    rows = jnp.concatenate([summed[:4], both[4:]], axis=0)
    return rows[:4], turned(rows)


def block_columns(rows, columns, b):
    cum_row = rows[b : b + 1]
    cum = columns[:, b : b + 1]
    rate = columns[:, 4 + b : 5 + b]
    first = lax.broadcasted_iota(jnp.int32, (128, 1), 0) < 64
    last = jnp.where(first, cum_row[:, 63:64], cum_row[:, 127:128])
    return cum_row, cum, rate, jnp.exp(cum), jnp.exp(last - cum)


def last_growth(rows, b):
    lane = lax.broadcasted_iota(jnp.int32, (1, 256), 1)
    return jnp.exp(jnp.where(lane < 128, rows[b : b + 1, 63:64], rows[b : b + 1, 127:128]))


def block_tables(query, key, rows, columns, b):
    row, col = iotas()
    causal = ((row >> 6) == (col >> 6)) & (row >= col)
    cum_row, cum, rate, _, _ = block_columns(rows, columns, b)
    within = jnp.where(causal, jnp.exp(jnp.where(causal, cum - cum_row, 0.0)), 0.0)
    key2 = twice(key)
    strict = jnp.where(row > col, within, 0.0) * rate
    system = strict * dot3(key2, key2, "nt")
    query_key = dot3(twice(query), key2, "nt") * within
    return within, system, query_key


def inverse(systems):
    row, col = iotas()
    found = None
    for level in range(6):
        here = ((row >> (level + 1)) == (col >> (level + 1))) & ((row >> level) != (col >> level))
        below = [jnp.where(here, system, 0.0) for system in systems]
        if found is None:
            eye = jnp.where(row == col, 1.0, 0.0).astype(F32)
            found = [eye - one for one in below]
        else:
            half = [dot3(one, two) for one, two in zip(found, below)]
            found = [one - dot3(two, one) for one, two in zip(found, half)]
    return found


def gated(out, gate):
    inv = lax.rsqrt(jnp.mean(out * out, axis=-1, keepdims=True) + EPS)
    return out * inv * (gate / (1.0 + jnp.exp(-gate)))


def gated_back(out, gate, grad):
    inv = lax.rsqrt(jnp.mean(out * out, axis=-1, keepdims=True) + EPS)
    sig = 1.0 / (1.0 + jnp.exp(-gate))
    weighted = grad * (gate * sig)
    grad_gate = grad * out * inv * (sig * (1.0 + gate * (1.0 - sig)))
    along = jnp.mean(weighted * out, axis=-1, keepdims=True)
    return inv * (weighted - out * (inv * inv * along)), grad_gate


def block_grads(
    query, key, value, cols, growth_last, tables, step, update, grad_out, grad_state, state_in
):
    _, _, rate, growth, remain = cols
    within, system, query_key = tables
    row, col = iotas()
    key2, query2 = twice(key), twice(query)
    grad_scores = dot3(grad_out, update, "nt")
    grad_system = -dot(step, update, "nt")
    masked = grad_scores * within
    strict = jnp.where(row > col, grad_system * within, 0.0) * rate
    pulled = grad_system * system
    spread = grad_scores * query_key + pulled
    grad_query = fold(dot(masked, key2))
    state_key = dot(diagonal_heads(update), grad_state, "nt")
    grad_key = fold(
        dot(masked, query2, "tn") + dot(strict, key2) + dot(strict, key2, "tn") + remain * state_key
    )
    tail = remain * jnp.sum(key2 * state_key, axis=-1, keepdims=True)
    grad_cum = jnp.sum(spread, axis=-1, keepdims=True) - tail
    grad_row = -jnp.sum(spread, axis=0, keepdims=True)
    end0 = jnp.sum(tail[:64], axis=0, keepdims=True)
    end1 = jnp.sum(tail[64:], axis=0, keepdims=True)
    grad_value = rate * step
    if state_in is None:
        inner = value
    else:
        state, key_state, query_state = state_in
        inner = value - growth * key_state
        out_growth = growth * grad_out
        in_growth = growth * grad_value
        grad_cum += jnp.sum(out_growth * query_state - in_growth * key_state, axis=-1, keepdims=True)
        grad_query += dot3(side_heads(out_growth), state, "nt")
        grad_key -= dot(side_heads(in_growth), state, "nt")
        kept = jnp.sum(growth_last * (state * grad_state), axis=0, keepdims=True)
        end0 += jnp.sum(kept[:, :128], axis=1, keepdims=True)
        end1 += jnp.sum(kept[:, 128:], axis=1, keepdims=True)
    lane = lax.broadcasted_iota(jnp.int32, (1, 128), 1)
    grad_row += jnp.where(lane == 63, end0, 0.0) + jnp.where(lane == 127, end1, 0.0)
    grad_rate = jnp.sum(step * inner, axis=-1, keepdims=True) + (
        jnp.sum(pulled, axis=-1, keepdims=True) / rate
    )
    return grad_query, grad_key, grad_value, grad_rate, grad_cum, grad_row


def decay_grads(grad_cums, grad_rates, grad_rows):
    row, col = iotas()
    packed = jnp.zeros((128, 128), F32)
    for b in range(4):
        packed = jnp.where(col == b, grad_cums[b], packed)
        packed = jnp.where(col == 4 + b, grad_rates[b], packed)
    packed = jnp.transpose(packed)[:8]
    since = jnp.where(((row >> 6) == (col >> 6)) & (row >= col), 1.0, 0.0).astype(F32)
    grad_cum = packed[:4] + jnp.concatenate(grad_rows, axis=0)
    grad_cum = jnp.concatenate([grad_cum, jnp.zeros((4, 128), F32)], axis=0)
    return by_head(packed[4:]), by_head(dot_exact(grad_cum, since)[:4])


BACK, APART, FLAGS = 32, 64, 80


def plan_kernel(response_ref, owner_ref, plan_ref, home_s):
    me = lax.axis_index("seq")
    chip, core = me // 2, me % 2

    def find_home(response, home):
        following = jnp.minimum(home + 1, N_SEQ - 1)
        here = (home < N_SEQ - 1) & (response_ref[3 * following] <= response)
        home = jnp.where(here, following, home)
        home_s[response] = home
        return home

    lax.fori_loop(0, 2 * N_SEQ, find_home, jnp.int32(0))

    def plan(offset, carry):
        to = 2 * ((chip + offset) % CHIPS) + core
        first = response_ref[3 * to] >> 1
        for slot in range(2):
            owner = owner_ref[jnp.minimum(first + slot, N_SEQ - 1)]
            plan_ref[2 * offset + slot] = (me - owner + 31) % N_SEQ
        prompt = jnp.int32(0)
        for candidate in range(N_SEQ):
            prompt = jnp.where(owner_ref[candidate] == to, candidate, prompt)
        homes = [home_s[2 * prompt + j] for j in range(2)]
        for j, home in enumerate(homes):
            slot = prompt - (response_ref[3 * home] >> 1)
            plan_ref[BACK + 2 * offset + j] = 2 * ((me - home + 31) % N_SEQ) + slot
        plan_ref[APART + offset] = jnp.where(homes[0] != homes[1], 1, 0)
        return carry

    lax.fori_loop(0, CHIPS, plan, 0)
    own = [response_ref[3 * me + j] for j in range(3)]
    for j in (1, 2):
        plan_ref[FLAGS + j - 1] = jnp.where(own[j] != own[j - 1], 1, 0)
        plan_ref[FLAGS + 1 + j] = jnp.where((own[j] >> 1) != (own[0] >> 1), 1, 0)


def rows_of(index, size):
    return pl.ds(pl.multiple_of(index * size, size), size)


def send(src, dst, send_sem, recv_sem, device):
    copy = pltpu.make_async_remote_copy(
        src_ref=src,
        dst_ref=dst,
        send_sem=send_sem,
        recv_sem=recv_sem,
        device_id=device,
        device_id_type=MESH,
    )
    copy.start()


def await_bytes(ref, sem):
    pltpu.make_async_copy(ref, ref, sem).wait()


def layer_kernel(
    query_ref,
    key_ref,
    value_ref,
    gate_ref,
    rate_ref,
    decay_ref,
    weight_ref,
    cot_ref,
    plan_ref,
    layer_ref,
    grad_query_ref,
    grad_key_ref,
    grad_value_ref,
    grad_gate_ref,
    grad_rate_ref,
    grad_decay_ref,
    grad_weight_ref,
    cots,
    piece_src,
    pieces,
    chosen_src,
    chosen,
    starts,
    grad_src,
    grad_pieces,
    owned_src,
    owned,
    sums_src,
    sums,
    weight_src,
    weight_pair,
    weight_sum,
    weight_in,
    within_s,
    system_s,
    scores_s,
    inverse_s,
    outs_s,
    update_s,
    step_s,
    grad_out_s,
    state_s,
    grad_state_s,
    key_state_s,
    query_state_s,
    normed_s,
    ring_send,
    ring_recv,
    sum_send,
    sum_recv,
    seq_send,
    seq_recv,
):
    me = lax.axis_index("seq")
    head = lax.axis_index("head")
    chip, core = me // 2, me % 2
    right, left = (head + 1) % N_HEAD, (head + N_HEAD - 1) % N_HEAD

    barrier = pltpu.get_barrier_semaphore()

    def greet(offset, carry):
        pl.semaphore_signal(
            barrier, inc=1, device_id={"seq": (me + offset) % N_SEQ}, device_id_type=MESH
        )
        return carry

    lax.fori_loop(1, N_SEQ, greet, 0)
    for neighbour in (left, right):
        pl.semaphore_signal(barrier, inc=1, device_id={"head": neighbour}, device_id_type=MESH)
    pl.semaphore_wait(barrier, N_SEQ + 1)

    def ring_piece(hop, to_right):
        if hop == 4:
            return cots.at[3, pl.ds(0 if to_right else 128, 128)]
        return cots.at[hop - 1 if to_right else 3 + hop]

    def ring_start(hop):
        for to_right in (True, False):
            if hop == 1:
                src = cot_ref
            else:
                src = cots.at[hop - 2 if to_right else 2 + hop]
                if hop == 4:
                    src = src.at[pl.ds(0 if to_right else 128, 128)]
            index = 2 * (hop - 1) + (0 if to_right else 1)
            send(
                src,
                ring_piece(hop, to_right),
                ring_send.at[index],
                ring_recv.at[index],
                {"head": right if to_right else left},
            )

    def ring_arrived(hop):
        for to_right in (True, False):
            index = 2 * (hop - 1) + (0 if to_right else 1)
            await_bytes(ring_piece(hop, to_right), ring_recv.at[index])

    ring_start(1)

    rate2, decay2 = rate_ref[...], decay_ref[...]
    rows, columns = running_decay(rate2, decay2)

    def unit_block(ref, b):
        raw = ref[SPAN * b : SPAN * b + SPAN, :].astype(F32)
        return raw * unit_scale(raw)

    def block_of(ref, b):
        return stack_heads(ref[SPAN * b : SPAN * b + SPAN, :]).astype(F32)

    queries = [unit_block(query_ref, b) * SCALE for b in range(4)]
    keys = [unit_block(key_ref, b) for b in range(4)]
    cols = [block_columns(rows, columns, b) for b in range(4)]

    def tables_of(b):
        within, system, query_key = block_tables(queries[b], keys[b], rows, columns, b)
        within_s[b] = within
        system_s[b] = system
        scores_s[b] = query_key
        return system

    def tail_of(b):
        return twice(keys[b]) * cols[b][4]

    inverse_s[0] = inverse([tables_of(0)])[0].astype(BF16)
    update = dot(inverse_s[0], cols[0][2] * block_of(value_ref, 0))
    update_s[0] = update
    final = dot(tail_of(0), diagonal_heads(update), "tn")
    piece_src[0:128, :] = final[:, :128].astype(BF16)
    piece_src[128:256, :] = final[:, 128:].astype(BF16)

    def send_pieces(offset, carry):
        to = (me + offset) % N_SEQ
        send(
            piece_src.at[rows_of(to // 2, 16)],
            pieces.at[offset - 1],
            seq_send.at[0],
            seq_recv.at[0],
            {"seq": to},
        )
        return carry

    lax.fori_loop(1, N_SEQ, send_pieces, 0)
    pieces[31] = piece_src[rows_of(chip, 16), :]

    ring_arrived(1)
    ring_start(2)
    for b, found in zip((1, 2, 3), inverse([tables_of(b) for b in (1, 2, 3)])):
        inverse_s[b] = found.astype(BF16)

    await_bytes(pieces.at[pl.ds(0, 31)], seq_recv.at[0])

    def choose(offset):
        return [pieces[plan_ref[2 * offset + slot]] for slot in range(2)]

    def send_chosen(offset, carry):
        for slot, piece in enumerate(choose(offset)):
            chosen_src[pl.ds(pl.multiple_of((offset - 1) * 32 + 16 * slot, 16), 16), :] = piece
        send(
            chosen_src.at[rows_of(offset - 1, 32)],
            chosen.at[rows_of(offset - 1, 32)],
            seq_send.at[1],
            seq_recv.at[1],
            {"seq": 2 * ((chip + offset) % CHIPS) + core},
        )
        return carry

    lax.fori_loop(1, CHIPS, send_chosen, 0)
    for slot, piece in enumerate(choose(0)):
        chosen[480 + 16 * slot : 496 + 16 * slot, :] = piece

    ring_arrived(2)
    ring_start(3)

    def norm_block(b, out):
        outs_s[b] = out
        result = side_heads(gated(out, block_of(gate_ref, b))).astype(BF16)
        normed_s[SPAN * b : SPAN * b + SPAN, :] = result

    norm_block(0, dot3(scores_s[0], update_s[0]))

    await_bytes(chosen.at[pl.ds(0, 480)], seq_recv.at[1])
    for slot in range(2):
        for piece in range(CHIPS):
            place = (chip - piece + 15) % CHIPS
            starts[slot, 16 * (piece % 8) : 16 * (piece % 8) + 16, 128 * (piece // 8) : 128 * (piece // 8) + 128] = (
                chosen[pl.ds(pl.multiple_of(place * 32 + 16 * slot, 16), 16), :].astype(F32)
            )
    ring_arrived(3)
    ring_start(4)

    fresh = [None, None] + [plan_ref[FLAGS + b].astype(F32) for b in range(2)]
    later = [None, None] + [plan_ref[FLAGS + 2 + b].astype(F32) for b in range(2)]

    state = None
    for b in (1, 2, 3):
        if b == 1:
            state = starts[0]
        else:
            begun = (1.0 - later[b]) * starts[0] + later[b] * starts[1]
            state = fresh[b] * begun + (1.0 - fresh[b]) * state
        state_s[b - 1] = state
        _, _, rate, growth, _ = cols[b]
        both = dot3(jnp.concatenate([keys[b], queries[b]], axis=0), state)
        key_state, query_state = stack_heads(both[:64]), stack_heads(both[64:])
        key_state_s[b - 1] = key_state
        query_state_s[b - 1] = query_state
        update = dot(inverse_s[b], rate * (block_of(value_ref, b) - growth * key_state))
        update_s[b] = update
        if b < 3:
            state = last_growth(rows, b) * state + dot(tail_of(b), diagonal_heads(update), "tn")
        norm_block(b, growth * query_state + dot3(scores_s[b], update))

    def share(distance):
        block = (head + distance + N_HEAD) % N_HEAD
        return dot(normed_s[...], weight_ref[rows_of(block, 256), :], "nt")

    def sums_start(hop):
        for to_right in (True, False):
            index = 2 * (hop - 1) + (0 if to_right else 1)
            if hop == 1:
                half = pl.ds(0 if to_right else 128, 128)
                block = (head + 4) % N_HEAD
                sums_src[index, half, :] = dot(
                    normed_s[half, :], weight_ref[rows_of(block, 256), :], "nt"
                ).astype(BF16)
                src, dst = sums_src.at[index, half], sums.at[index, half]
            else:
                total = share(5 - hop if to_right else hop - 5)
                if hop == 2:
                    low = 0 if to_right else 128
                    sums_src[index] = total.astype(BF16)
                    sums_src[index, low : low + 128, :] = (
                        total[low : low + 128] + sums[index - 2, low : low + 128, :].astype(F32)
                    ).astype(BF16)
                else:
                    sums_src[index] = (total + sums[index - 2].astype(F32)).astype(BF16)
                src, dst = sums_src.at[index], sums.at[index]
            send(
                src,
                dst,
                sum_send.at[index],
                sum_recv.at[index],
                {"head": right if to_right else left},
            )

    def sums_piece(hop, to_right):
        index = 2 * (hop - 1) + (0 if to_right else 1)
        if hop == 1:
            return sums.at[index, pl.ds(0 if to_right else 128, 128)]
        return sums.at[index]

    def sums_arrived(hop):
        for to_right in (True, False):
            await_bytes(
                sums_piece(hop, to_right), sum_recv.at[2 * (hop - 1) + (0 if to_right else 1)]
            )

    sums_start(1)

    ring_arrived(4)

    def cot_slots():
        yield cot_ref, head
        for hop in (1, 2, 3, 4):
            yield cots.at[hop - 1], (head - hop + N_HEAD) % N_HEAD
        for hop in (1, 2, 3):
            yield cots.at[3 + hop], (head + hop) % N_HEAD

    grad_normed = None
    for slot_ref, block in cot_slots():
        term = dot(slot_ref[...], weight_ref[rows_of(block, 256), :])
        grad_normed = term if grad_normed is None else grad_normed + term
    for b in range(4):
        grad_out, grad_gate = gated_back(
            outs_s[b], block_of(gate_ref, b), stack_heads(grad_normed[SPAN * b : SPAN * b + SPAN])
        )
        grad_out_s[b] = grad_out
        grad_gate_ref[SPAN * b : SPAN * b + SPAN, :] = side_heads(grad_gate)

    grad_state = jnp.zeros((128, 256), F32)
    begun = [jnp.zeros((128, 256), F32), jnp.zeros((128, 256), F32)]
    for b in (3, 2, 1):
        _, _, rate, growth, remain = cols[b]
        grad_out = grad_out_s[b]
        grad_state_s[b] = grad_state
        grad_update = dot(scores_s[b], grad_out, "tn")
        if b < 3:
            grad_update += remain * stack_heads(dot(keys[b], grad_state))
        step = dot(inverse_s[b], grad_update, "tn")
        step_s[b] = step
        sides = jnp.concatenate(
            [side_heads(-(rate * growth) * step), side_heads(growth * grad_out)], axis=0
        )
        grad_in = dot(jnp.concatenate([keys[b], queries[b]], axis=0), sides, "tn")
        if b < 3:
            grad_in += last_growth(rows, b) * grad_state
        if b > 1:
            begun[0] += (fresh[b] * (1.0 - later[b])) * grad_in
            begun[1] += (fresh[b] * later[b]) * grad_in
            grad_state = (1.0 - fresh[b]) * grad_in
        else:
            begun[0] += grad_in
    for slot in range(2):
        for piece in range(CHIPS):
            grad_src[2 * piece + slot] = begun[slot][
                16 * (piece % 8) : 16 * (piece % 8) + 16,
                128 * (piece // 8) : 128 * (piece // 8) + 128,
            ].astype(BF16)

    def send_grads(offset, carry):
        to = (me + offset) % N_SEQ
        send(
            grad_src.at[pl.ds(2 * (to // 2), 2)],
            grad_pieces.at[pl.ds(2 * (offset - 1), 2)],
            seq_send.at[2],
            seq_recv.at[2],
            {"seq": to},
        )
        return carry

    lax.fori_loop(1, N_SEQ, send_grads, 0)
    for slot in range(2):
        grad_pieces[62 + slot] = grad_src[2 * chip + slot]

    sums_arrived(1)
    sums_start(2)
    for slot_ref, block in cot_slots():
        share_w = dot(slot_ref[...], normed_s[...], "tn").astype(BF16)
        for quarter in range(4):
            place = (quarter % 2) * 1024 + (2 * block + quarter // 2) * 64
            weight_src[pl.ds(pl.multiple_of(place, 64), 64), :] = share_w[
                64 * quarter : 64 * quarter + 64
            ]
    send(
        weight_src.at[rows_of(1 - core, 1024)],
        weight_pair,
        seq_send.at[4],
        seq_recv.at[4],
        {"seq": 2 * chip + 1 - core},
    )

    await_bytes(grad_pieces.at[pl.ds(0, 62)], seq_recv.at[2])

    def owned_piece(offset):
        one = grad_pieces[plan_ref[BACK + 2 * offset]].astype(F32)
        two = grad_pieces[plan_ref[BACK + 2 * offset + 1]].astype(F32)
        return (one + plan_ref[APART + offset].astype(F32) * two).astype(BF16)

    def send_owned(offset, carry):
        owned_src[rows_of(offset - 1, 16), :] = owned_piece(offset)
        send(
            owned_src.at[rows_of(offset - 1, 16)],
            owned.at[rows_of(offset - 1, 16)],
            seq_send.at[3],
            seq_recv.at[3],
            {"seq": 2 * ((chip + offset) % CHIPS) + core},
        )
        return carry

    lax.fori_loop(1, CHIPS, send_owned, 0)
    owned[240:256, :] = owned_piece(0)

    await_bytes(weight_pair, seq_recv.at[4])
    for part in range(4):
        place = core * 1024 + 256 * part
        weight_sum[256 * part : 256 * part + 256, :] = (
            weight_src[pl.ds(pl.multiple_of(place, 256), 256), :].astype(F32)
            + weight_pair[256 * part : 256 * part + 256, :].astype(F32)
        ).astype(BF16)

    def send_weight(offset, carry):
        to = (chip + offset) % CHIPS
        send(
            weight_sum.at[rows_of(to, 64)],
            weight_in.at[rows_of(offset - 1, 64)],
            seq_send.at[5],
            seq_recv.at[5],
            {"seq": 2 * to + core},
        )
        return carry

    lax.fori_loop(1, CHIPS, send_weight, 0)
    sums_arrived(2)
    sums_start(3)

    grad_cums, grad_rates, grad_rows = [None] * 4, [None] * 4, [None] * 4

    def finish_block(b, grad_state, state_in):
        tables = (within_s[b], system_s[b], scores_s[b])
        found = block_grads(
            queries[b],
            keys[b],
            block_of(value_ref, b),
            cols[b],
            last_growth(rows, b),
            tables,
            step_s[b],
            update_s[b],
            grad_out_s[b],
            grad_state,
            state_in,
        )
        grad_query_ref[SPAN * b : SPAN * b + SPAN, :] = found[0]
        grad_key_ref[SPAN * b : SPAN * b + SPAN, :] = found[1]
        grad_value_ref[SPAN * b : SPAN * b + SPAN, :] = side_heads(found[2])
        grad_rates[b], grad_cums[b], grad_rows[b] = found[3:]

    for b in (1, 2, 3):
        finish_block(b, grad_state_s[b], (state_s[b - 1], key_state_s[b - 1], query_state_s[b - 1]))
        if b == 2:
            sums_arrived(3)
            sums_start(4)

    await_bytes(owned.at[pl.ds(0, 240)], seq_recv.at[3])
    for piece in range(CHIPS):
        place = (chip - piece + 15) % CHIPS
        grad_state_s[0, 16 * (piece % 8) : 16 * (piece % 8) + 16, 128 * (piece // 8) : 128 * (piece // 8) + 128] = (
            owned[rows_of(place, 16), :].astype(F32)
        )
    grad_state = grad_state_s[0]
    grad_update = dot(scores_s[0], grad_out_s[0], "tn")
    grad_update += cols[0][4] * stack_heads(dot(keys[0], grad_state))
    step_s[0] = dot(inverse_s[0], grad_update, "tn")
    finish_block(0, grad_state, None)
    grad_rate_ref[...], grad_decay_ref[...] = decay_grads(grad_cums, grad_rates, grad_rows)

    await_bytes(weight_in.at[pl.ds(0, 15 * 64)], seq_recv.at[5])
    total = weight_sum[rows_of(chip, 64), :].astype(F32)
    for slot in range(15):
        total += weight_in[64 * slot : 64 * slot + 64, :].astype(F32)
    grad_weight_ref[...] = total
    total = share(0)
    sums_arrived(4)
    layer_ref[...] = (total + sums[6].astype(F32) + sums[7].astype(F32)).astype(BF16)

    for hop in (1, 2, 3, 4):
        for to_right in (True, False):
            index = 2 * (hop - 1) + (0 if to_right else 1)
            await_bytes(ring_piece(hop, to_right), ring_send.at[index])
            await_bytes(sums_piece(hop, to_right), sum_send.at[index])
    await_bytes(pieces.at[pl.ds(0, 31)], seq_send.at[0])
    await_bytes(chosen.at[pl.ds(0, 480)], seq_send.at[1])
    await_bytes(grad_pieces.at[pl.ds(0, 62)], seq_send.at[2])
    await_bytes(owned.at[pl.ds(0, 240)], seq_send.at[3])
    await_bytes(weight_pair, seq_send.at[4])
    await_bytes(weight_in.at[pl.ds(0, 15 * 64)], seq_send.at[5])


SCRATCH = [
    pltpu.VMEM((7, 256, 256), BF16),
    pltpu.VMEM((256, 128), BF16),
    pltpu.VMEM((32, 16, 128), BF16),
    pltpu.VMEM((480, 128), BF16),
    pltpu.VMEM((512, 128), BF16),
    pltpu.VMEM((2, 128, 256), F32),
    pltpu.VMEM((32, 16, 128), BF16),
    pltpu.VMEM((64, 16, 128), BF16),
    pltpu.VMEM((240, 128), BF16),
    pltpu.VMEM((256, 128), BF16),
    pltpu.VMEM((8, 256, 256), BF16),
    pltpu.VMEM((8, 256, 256), BF16),
    pltpu.VMEM((2048, 256), BF16),
    pltpu.VMEM((1024, 256), BF16),
    pltpu.VMEM((1024, 256), BF16),
    pltpu.VMEM((960, 256), BF16),
    pltpu.VMEM((4, 128, 128), F32),
    pltpu.VMEM((4, 128, 128), F32),
    pltpu.VMEM((4, 128, 128), F32),
    pltpu.VMEM((4, 128, 128), BF16),
    pltpu.VMEM((4, 128, 128), F32),
    pltpu.VMEM((4, 128, 128), F32),
    pltpu.VMEM((4, 128, 128), F32),
    pltpu.VMEM((4, 128, 128), F32),
    pltpu.VMEM((3, 128, 256), F32),
    pltpu.VMEM((4, 128, 256), F32),
    pltpu.VMEM((3, 128, 128), F32),
    pltpu.VMEM((3, 128, 128), F32),
    pltpu.VMEM((256, 256), BF16),
    pltpu.SemaphoreType.DMA((8,)),
    pltpu.SemaphoreType.DMA((8,)),
    pltpu.SemaphoreType.DMA((8,)),
    pltpu.SemaphoreType.DMA((8,)),
    pltpu.SemaphoreType.DMA((6,)),
    pltpu.SemaphoreType.DMA((6,)),
]


def unit_back(raw, grad, scale):
    inv = unit_scale(raw)
    unit = raw * inv
    return (scale * inv) * (grad - unit * jnp.sum(grad * unit, axis=-1, keepdims=True))


def finish_kernel(
    query_ref, key_ref, layer, query, key, value, gate, rate, decay, weight,
    layer_out, query_out, key_out, value_out, gate_out, rate_out, decay_out, weight_out,
):
    layer_out[...] = layer[...]
    query_out[...] = unit_back(query_ref[...].astype(F32), query[...], SCALE)
    key_out[...] = unit_back(key_ref[...].astype(F32), key[...], 1.0)
    value_out[...] = value[...]
    gate_out[...] = gate[...]
    rate_out[...] = rate[...]
    decay_out[...] = decay[...]
    weight_out[...] = weight[...]


RESULTS = [
    jax.ShapeDtypeStruct((256, 256), BF16),
    jax.ShapeDtypeStruct((256, 128), F32),
    jax.ShapeDtypeStruct((256, 128), F32),
    jax.ShapeDtypeStruct((256, 256), F32),
    jax.ShapeDtypeStruct((256, 256), F32),
    jax.ShapeDtypeStruct((2, 256), F32),
    jax.ShapeDtypeStruct((2, 256), F32),
    jax.ShapeDtypeStruct((64, 256), F32),
]


def per_device(
    query_rows, key_rows, value_rows, output_gate, write_rate, log_decay,
    out_weight, out_cotangent, block_response, prefix_owner,
):
    vmem = pl.BlockSpec(memory_space=pltpu.VMEM)
    smem = pl.BlockSpec(memory_space=pltpu.SMEM)
    plan = pl.pallas_call(
        plan_kernel,
        out_shape=jax.ShapeDtypeStruct((96,), jnp.int32),
        in_specs=[smem] * 2,
        out_specs=smem,
        scratch_shapes=[pltpu.SMEM((64,), jnp.int32)],
    )(block_response, prefix_owner)
    results = pl.pallas_call(
        layer_kernel,
        out_shape=RESULTS,
        in_specs=[vmem] * 8 + [smem],
        out_specs=[vmem] * 8,
        scratch_shapes=SCRATCH,
        compiler_params=pltpu.CompilerParams(
            collective_id=0, has_side_effects=True, vmem_limit_bytes=48 * 1024 * 1024
        ),
    )(
        query_rows, key_rows, value_rows, output_gate, write_rate, log_decay,
        out_weight, out_cotangent, plan,
    )
    return pl.pallas_call(
        finish_kernel,
        out_shape=RESULTS,
        in_specs=[vmem] * 10,
        out_specs=[vmem] * 8,
    )(query_rows, key_rows, *results)


def solution(mesh):
    rows = P("seq", "head")
    return jax.shard_map(
        per_device,
        mesh=mesh,
        in_specs=(rows, rows, rows, rows, P("head", "seq"), P("head", "seq"), P(None, "head"), rows, P(), P()),
        out_specs=(rows, rows, rows, rows, rows, P("head", "seq"), P("head", "seq"), rows),
        check_vma=False,
    )
```

time: 299 us -> 66 us (0.22); the launches traced: 295 us -> 65.3 us
  other arithmetic: 94 us -> 0 us
  matrix products: 75.5 us -> 0 us
  Pallas kernels: 0 us -> 52.5 us
  local copies, waits for them, and re-layouts: 47.7 us -> 12.2 us
  starting transfers between devices: 29.1 us -> 0 us
  waiting for transfers between devices: 26.8 us -> 0 us
  between operations: 15.5 us -> 0.68 us
  loops' own time: 6.3 us -> 0 us
    dot_general x74 -> x0, matrix products: 69.5 us -> none  [the longest x11 16.7 us: span_apply(): jnp.einsum('...ck,...vk->...cv', weights_w, state_in, precision=highest)]
    pallas_call x0 -> x3, Pallas kernels: none -> 52.5 us  [the longest x1 47.2 us: per_device(): pl.pallas_call(layer_kernel, out_shape=RESULTS, in_specs=[vmem] * 8 + [sm...]
    another operation x10 -> x0, other arithmetic: 46.3 us -> none  [the longest x4 40.8 us: span_parts(): lax.linalg.triangular_solve(system, right_side, left_side=True, lower=Tru...]
    all_to_all x4 -> x0, starting transfers between devices: 29.1 us -> none  [the longest x2 17.4 us: sent_to_all(): lax.all_to_all(jnp.broadcast_to(x[None], (peers, *x.shape)), axis, 0, 0,...]
    all_to_all x4 -> x0, waiting for transfers between devices: 26.1 us -> none  [the longest x2 18 us: sent_to_all(): lax.all_to_all(jnp.broadcast_to(x[None], (peers, *x.shape)), axis, 0, 0,...]
    convert_element_type x8 -> x0, other arithmetic: 12 us -> none  [the longest x1 4.04 us: per_device(): states_all = shared.astype(jnp.float32)]
    unnamed x166 -> x34, local copies, waits for them, and re-layouts: 2.51 us -> 12.2 us
    reduce_sum x21 -> x0, other arithmetic: 9.29 us -> none  [the longest x4 2.24 us: unit_rows(): raw_rows * lax.rsqrt(jnp.sum(raw_rows * raw_rows, axis=-1, keepdims=True)...]
  transfers between devices with their start and end apart: 5 -> 0, of which waited for: 3 -> 0; matrix products, arithmetic and copies ran while one was open for 45% -> 0% of each run, Pallas kernels for 0% -> 0%
where the time goes in v1:
time: 66 us; the launch traced here: 65.3 us
  Pallas kernels  52.5 us (80%)
  local copies, waits for them, and re-layouts  12.2 us (18%)
  between operations  0.68 us (1%)
    pallas_call x1, Pallas kernels, per_device(): pl.pallas_call(layer_kernel, out_shape=RESULTS, in_specs=[vmem] * 8 + [sm...  47.2 us
    unnamed x34, local copies, waits for them, and re-layouts  12.2 us
    pallas_call x1, Pallas kernels, per_device(): pl.pallas_call(plan_kernel, out_shape=jax.ShapeDtypeStruct((96,), jnp.int...  2.93 us
    pallas_call x1, Pallas kernels, per_device(): pl.pallas_call(finish_kernel, out_shape=RESULTS, in_specs=[vmem] * 10, ou...  2.39 us

profile of v1, /device:TPU:1, one launch (start us, length us, event | category | flops | bytes accessed | tf_op | source)
XLA Modules:
  0.0 65.3 jit_solution(15986717803014613128)
XLA Ops:
  0.6 2.9 %shard_map.161.plan_ref = s32[96]{0:T(128)} custom-call(s32[96]{0:T(128)} %response_ref.1, s32[32]{0:T(128)} %owner_ref.1), custom_call_target="tpu_custom_call" | custom-call | tf_op jit(solution)/shard_map/pallas_call | solution.py:816
  3.6 0.0 copy-start
  3.6 1.2 %copy-done = bf16[2048,256]{1,0:T(8,128)(2,1)S(1)} copy-done((bf16[2048,256]{1,0:T(8,128)(2,1)S(1)}, bf16[2048,256]{1,0:T(8,128)(2,1)}, u32[]{:S(2)}) %copy-start) | copy-done | bytes 1048600
  4.8 0.0 copy-start.3
  4.8 0.8 %copy-done.3 = bf16[256,128]{1,0:T(8,128)(2,1)S(1)} copy-done((bf16[256,128]{1,0:T(8,128)(2,1)S(1)}, bf16[256,128]{1,0:T(8,128)(2,1)}, u32[]{:S(2)}) %copy-start.3) | copy-done | bytes 65560
  5.6 0.0 copy-start.4
  5.6 0.8 %copy-done.4 = bf16[256,128]{1,0:T(8,128)(2,1)S(1)} copy-done((bf16[256,128]{1,0:T(8,128)(2,1)S(1)}, bf16[256,128]{1,0:T(8,128)(2,1)}, u32[]{:S(2)}) %copy-start.4) | copy-done | bytes 65560
  6.5 0.0 copy-start.5
  6.5 0.9 %copy-done.5 = bf16[256,256]{1,0:T(8,128)(2,1)S(1)} copy-done((bf16[256,256]{1,0:T(8,128)(2,1)S(1)}, bf16[256,256]{1,0:T(8,128)(2,1)}, u32[]{:S(2)}) %copy-start.5) | copy-done | bytes 131096
  7.4 0.0 copy-start.6
  7.4 0.9 %copy-done.6 = bf16[256,256]{1,0:T(8,128)(2,1)S(1)} copy-done((bf16[256,256]{1,0:T(8,128)(2,1)S(1)}, bf16[256,256]{1,0:T(8,128)(2,1)}, u32[]{:S(2)}) %copy-start.6) | copy-done | bytes 131096
  8.3 0.0 copy-start.7
  8.3 0.9 %copy-done.7 = bf16[256,256]{1,0:T(8,128)(2,1)S(1)} copy-done((bf16[256,256]{1,0:T(8,128)(2,1)S(1)}, bf16[256,256]{1,0:T(8,128)(2,1)}, u32[]{:S(2)}) %copy-start.7) | copy-done | bytes 131096
  9.2 0.0 copy-start.12
  9.2 0.7 %copy-done.12 = f32[2,256]{1,0:T(2,128)S(1)} copy-done((f32[2,256]{1,0:T(2,128)S(1)}, f32[2,256]{1,0:T(2,128)}, u32[]{:S(2)}) %copy-start.12) | copy-done | bytes 2072
  9.9 0.0 copy-start.13
  9.9 0.7 %copy-done.13 = f32[2,256]{1,0:T(2,128)S(1)} copy-done((f32[2,256]{1,0:T(2,128)S(1)}, f32[2,256]{1,0:T(2,128)}, u32[]{:S(2)}) %copy-start.13) | copy-done | bytes 2072
  10.6 0.0 copy-start.16
  10.6 0.7 %copy-done.16 = s32[96]{0:T(128)S(1)} copy-done((s32[96]{0:T(128)S(1)}, s32[96]{0:T(128)}, u32[]{:S(2)}) %copy-start.16) | copy-done | bytes 408
  11.2 47.2 %shard_map.162 = (bf16[256,256]{1,0:T(8,128)(2,1)S(1)}, f32[256,128]{1,0:T(8,128)S(1)}, f32[256,128]{1,0:T(8,128)S(1)}, f32[256,256]{1,0:T(8,128)S(1)}, f32[256,...) custom-call(bf16[256,128]{1,0:T(8,128)(2,1)S(1)} %copy-done.3, ...), custom_call_target="tpu_custom_call" | custom-call | tf_op jit(solution)/shard_map/pallas_call | solution.py:823
  58.4 0.0 copy-start.1
  58.4 0.7 %copy-done.1 = f32[256,256]{1,0:T(8,128)} copy-done((f32[256,256]{1,0:T(8,128)}, f32[256,256]{1,0:T(8,128)S(1)}, u32[]{:S(2)}) %copy-start.1) | copy-done | bytes 262168
  59.1 0.0 copy-start.2
  59.1 0.7 %copy-done.2 = f32[256,256]{1,0:T(8,128)} copy-done((f32[256,256]{1,0:T(8,128)}, f32[256,256]{1,0:T(8,128)S(1)}, u32[]{:S(2)}) %copy-start.2) | copy-done | bytes 262168
  59.8 0.0 copy-start.8
  59.8 0.6 copy-done.8
  60.4 0.0 copy-start.9
  60.4 0.6 copy-done.9
  61.1 0.0 copy-start.10
  61.1 0.6 copy-done.10
  61.7 0.0 copy-start.11
  61.7 0.6 copy-done.11
  62.3 0.0 copy-start.14
  62.3 0.0 copy-start.15
  62.3 0.6 copy-done.14
  62.9 0.0 copy-done.15
  62.9 2.4 %shard_map.163 = (bf16[256,256]{1,0:T(8,128)(2,1)}, f32[256,128]{1,0:T(8,128)}, f32[256,128]{1,0:T(8,128)}, f32[256,256]{1,0:T(8,128)}, f32[256,256]{1,0:T(8,128...) custom-call(bf16[256,128]{1,0:T(8,128)(2,1)} %query_ref.3, bf16[256,128]{1,0:T(8,128)(2,1)} %key_ref.3, ...), custom_call_target="tpu_custom_call" | custom-call | tf_op jit(solution)/shard_map/pallas_call | solution.py:836
Async XLA Ops:
  3.6 1.2 %copy-start = (bf16[2048,256]{1,0:T(8,128)(2,1)S(1)}, bf16[2048,256]{1,0:T(8,128)(2,1)}, u32[]{:S(2)}) copy-start(bf16[2048,256]{1,0:T(8,128)(2,1)} %weight_ref.1) | copy-start | bytes 3145732
  4.8 0.8 %copy-start.3 = (bf16[256,128]{1,0:T(8,128)(2,1)S(1)}, bf16[256,128]{1,0:T(8,128)(2,1)}, u32[]{:S(2)}) copy-start(bf16[256,128]{1,0:T(8,128)(2,1)} %query_ref.3) | copy-start | bytes 196612
  5.6 0.8 %copy-start.4 = (bf16[256,128]{1,0:T(8,128)(2,1)S(1)}, bf16[256,128]{1,0:T(8,128)(2,1)}, u32[]{:S(2)}) copy-start(bf16[256,128]{1,0:T(8,128)(2,1)} %key_ref.3) | copy-start | bytes 196612
  6.5 0.9 %copy-start.5 = (bf16[256,256]{1,0:T(8,128)(2,1)S(1)}, bf16[256,256]{1,0:T(8,128)(2,1)}, u32[]{:S(2)}) copy-start(bf16[256,256]{1,0:T(8,128)(2,1)} %value_ref.1) | copy-start | bytes 393220
  7.4 0.9 %copy-start.6 = (bf16[256,256]{1,0:T(8,128)(2,1)S(1)}, bf16[256,256]{1,0:T(8,128)(2,1)}, u32[]{:S(2)}) copy-start(bf16[256,256]{1,0:T(8,128)(2,1)} %gate_ref.1) | copy-start | bytes 393220
  8.3 0.9 %copy-start.7 = (bf16[256,256]{1,0:T(8,128)(2,1)S(1)}, bf16[256,256]{1,0:T(8,128)(2,1)}, u32[]{:S(2)}) copy-start(bf16[256,256]{1,0:T(8,128)(2,1)} %cot_ref.1) | copy-start | bytes 393220
  9.2 0.7 %copy-start.12 = (f32[2,256]{1,0:T(2,128)S(1)}, f32[2,256]{1,0:T(2,128)}, u32[]{:S(2)}) copy-start(f32[2,256]{1,0:T(2,128)} %rate_ref.1) | copy-start | bytes 6148
  9.9 0.7 %copy-start.13 = (f32[2,256]{1,0:T(2,128)S(1)}, f32[2,256]{1,0:T(2,128)}, u32[]{:S(2)}) copy-start(f32[2,256]{1,0:T(2,128)} %decay_ref.1) | copy-start | bytes 6148
  10.6 0.7 %copy-start.16 = (s32[96]{0:T(128)S(1)}, s32[96]{0:T(128)}, u32[]{:S(2)}) copy-start(s32[96]{0:T(128)} %shard_map.161.plan_ref) | copy-start | bytes 1156
  58.4 0.7 %copy-start.1 = (f32[256,256]{1,0:T(8,128)}, f32[256,256]{1,0:T(8,128)S(1)}, u32[]{:S(2)}) copy-start(f32[256,256]{1,0:T(8,128)S(1)} %get-tuple-element.19.value) | copy-start | bytes 786436
  59.1 0.7 %copy-start.2 = (f32[256,256]{1,0:T(8,128)}, f32[256,256]{1,0:T(8,128)S(1)}, u32[]{:S(2)}) copy-start(f32[256,256]{1,0:T(8,128)S(1)} %get-tuple-element.20.gate) | copy-start | bytes 786436
  59.8 0.7 copy-start.8
  60.4 0.7 copy-start.9
  61.1 0.6 copy-start.10
  61.7 0.6 copy-start.11
  62.3 0.6 copy-start.14
  62.3 0.6 copy-start.15

commit v2 on v1

--- a/solution.py
+++ b/solution.py
@@ -102,6 +102,12 @@
 
 def unit_scale(x):
     return lax.rsqrt(jnp.sum(x * x, axis=-1, keepdims=True) + EPS)
+
+
+def unit_back(raw, grad, scale):
+    inv = unit_scale(raw)
+    unit = raw * inv
+    return (scale * inv) * (grad - unit * jnp.sum(grad * unit, axis=-1, keepdims=True))
 
 
 def running_decay(write_rate, log_decay):
@@ -227,45 +233,6 @@
     return by_head(packed[4:]), by_head(dot_exact(grad_cum, since)[:4])
 
 
-BACK, APART, FLAGS = 32, 64, 80
-
-
-def plan_kernel(response_ref, owner_ref, plan_ref, home_s):
-    me = lax.axis_index("seq")
-    chip, core = me // 2, me % 2
-
-    def find_home(response, home):
-        following = jnp.minimum(home + 1, N_SEQ - 1)
-        here = (home < N_SEQ - 1) & (response_ref[3 * following] <= response)
-        home = jnp.where(here, following, home)
-        home_s[response] = home
-        return home
-
-    lax.fori_loop(0, 2 * N_SEQ, find_home, jnp.int32(0))
-
-    def plan(offset, carry):
-        to = 2 * ((chip + offset) % CHIPS) + core
-        first = response_ref[3 * to] >> 1
-        for slot in range(2):
-            owner = owner_ref[jnp.minimum(first + slot, N_SEQ - 1)]
-            plan_ref[2 * offset + slot] = (me - owner + 31) % N_SEQ
-        prompt = jnp.int32(0)
-        for candidate in range(N_SEQ):
-            prompt = jnp.where(owner_ref[candidate] == to, candidate, prompt)
-        homes = [home_s[2 * prompt + j] for j in range(2)]
-        for j, home in enumerate(homes):
-            slot = prompt - (response_ref[3 * home] >> 1)
-            plan_ref[BACK + 2 * offset + j] = 2 * ((me - home + 31) % N_SEQ) + slot
-        plan_ref[APART + offset] = jnp.where(homes[0] != homes[1], 1, 0)
-        return carry
-
-    lax.fori_loop(0, CHIPS, plan, 0)
-    own = [response_ref[3 * me + j] for j in range(3)]
-    for j in (1, 2):
-        plan_ref[FLAGS + j - 1] = jnp.where(own[j] != own[j - 1], 1, 0)
-        plan_ref[FLAGS + 1 + j] = jnp.where((own[j] >> 1) != (own[0] >> 1), 1, 0)
-
-
 def rows_of(index, size):
     return pl.ds(pl.multiple_of(index * size, size), size)
 
@@ -287,6 +254,24 @@
 
 
 def layer_kernel(
+    query_hbm,
+    key_hbm,
+    value_hbm,
+    gate_hbm,
+    rate_hbm,
+    decay_hbm,
+    weight_hbm,
+    cot_hbm,
+    response_ref,
+    owner_ref,
+    layer_ref,
+    grad_query_ref,
+    grad_key_ref,
+    grad_value_ref,
+    grad_gate_ref,
+    grad_rate_ref,
+    grad_decay_ref,
+    grad_weight_ref,
     query_ref,
     key_ref,
     value_ref,
@@ -295,15 +280,6 @@
     decay_ref,
     weight_ref,
     cot_ref,
-    plan_ref,
-    layer_ref,
-    grad_query_ref,
-    grad_key_ref,
-    grad_value_ref,
-    grad_gate_ref,
-    grad_rate_ref,
-    grad_decay_ref,
-    grad_weight_ref,
     cots,
     piece_src,
     pieces,
@@ -333,6 +309,9 @@
     key_state_s,
     query_state_s,
     normed_s,
+    pick_s,
+    gather_s,
+    load_sem,
     ring_send,
     ring_recv,
     sum_send,
@@ -345,6 +324,24 @@
     chip, core = me // 2, me % 2
     right, left = (head + 1) % N_HEAD, (head + N_HEAD - 1) % N_HEAD
 
+    loads = [
+        pltpu.make_async_copy(src, dst, load_sem.at[index])
+        for index, (src, dst) in enumerate(
+            (
+                (rate_hbm, rate_ref),
+                (decay_hbm, decay_ref),
+                (key_hbm, key_ref),
+                (query_hbm, query_ref),
+                (value_hbm, value_ref),
+                (gate_hbm, gate_ref),
+                (cot_hbm, cot_ref),
+                (weight_hbm, weight_ref),
+            )
+        )
+    ]
+    for load in loads:
+        load.start()
+
     barrier = pltpu.get_barrier_semaphore()
 
     def greet(offset, carry):
@@ -366,7 +363,7 @@
     def ring_start(hop):
         for to_right in (True, False):
             if hop == 1:
-                src = cot_ref
+                src = cot_hbm
             else:
                 src = cots.at[hop - 2 if to_right else 2 + hop]
                 if hop == 4:
@@ -387,6 +384,8 @@
 
     ring_start(1)
 
+    for load in loads[:5]:
+        load.wait()
     rate2, decay2 = rate_ref[...], decay_ref[...]
     rows, columns = running_decay(rate2, decay2)
 
@@ -422,7 +421,7 @@
         to = (me + offset) % N_SEQ
         send(
             piece_src.at[rows_of(to // 2, 16)],
-            pieces.at[offset - 1],
+            pieces.at[rows_of(offset - 1, 16)],
             seq_send.at[0],
             seq_recv.at[0],
             {"seq": to},
@@ -430,21 +429,45 @@
         return carry
 
     lax.fori_loop(1, N_SEQ, send_pieces, 0)
-    pieces[31] = piece_src[rows_of(chip, 16), :]
+    pieces[496:512, :] = piece_src[rows_of(chip, 16), :]
 
     ring_arrived(1)
     ring_start(2)
     for b, found in zip((1, 2, 3), inverse([tables_of(b) for b in (1, 2, 3)])):
         inverse_s[b] = found.astype(BF16)
 
-    await_bytes(pieces.at[pl.ds(0, 31)], seq_recv.at[0])
-
-    def choose(offset):
-        return [pieces[plan_ref[2 * offset + slot]] for slot in range(2)]
+    def owner_of(device, slot):
+        prompt = (response_ref[3 * device] >> 1) + slot
+        found = owner_ref[jnp.minimum(prompt, N_SEQ - 1)]
+        return jnp.where(prompt < N_SEQ, found, -1)
+
+    row, col = iotas((32, 512))
+    source = (me + 31 - (col >> 4)) % N_SEQ
+    for place in range(CHIPS):
+        to = 2 * ((chip + place + 1) % CHIPS) + core
+        wanted = jnp.where(row < 16, owner_of(to, 0), owner_of(to, 1))
+        here = (source == wanted) & ((row & 15) == (col & 15))
+        pick_s[32 * place : 32 * place + 32, :] = jnp.where(here, 1.0, 0.0).astype(BF16)
+
+    for quarter in range(8):
+        columns_here = []
+        for place in range(4 * quarter, 4 * quarter + 4):
+            device = (me + 31 - place) % N_SEQ
+            columns_here.append((owner_of(device, 0), owner_of(device, 1)))
+        row, col = iotas((256, 128))
+        owner = jnp.full((256, 128), -1, jnp.int32)
+        for index, (one, two) in enumerate(columns_here):
+            owner = jnp.where((col >> 4) == 2 * index, one, owner)
+            owner = jnp.where((col >> 4) == 2 * index + 1, two, owner)
+        target = 2 * ((chip + 1 + (row >> 4)) % CHIPS) + core
+        here = (owner == target) & ((row & 15) == (col & 15))
+        gather_s[:, 128 * quarter : 128 * quarter + 128] = jnp.where(here, 1.0, 0.0).astype(BF16)
+
+    await_bytes(pieces.at[pl.ds(0, 496)], seq_recv.at[0])
+
+    chosen_src[...] = dot(pick_s[...], pieces[...]).astype(BF16)
 
     def send_chosen(offset, carry):
-        for slot, piece in enumerate(choose(offset)):
-            chosen_src[pl.ds(pl.multiple_of((offset - 1) * 32 + 16 * slot, 16), 16), :] = piece
         send(
             chosen_src.at[rows_of(offset - 1, 32)],
             chosen.at[rows_of(offset - 1, 32)],
@@ -455,11 +478,12 @@
         return carry
 
     lax.fori_loop(1, CHIPS, send_chosen, 0)
-    for slot, piece in enumerate(choose(0)):
-        chosen[480 + 16 * slot : 496 + 16 * slot, :] = piece
+    chosen[480:512, :] = chosen_src[480:512, :]
 
     ring_arrived(2)
     ring_start(3)
+
+    loads[5].wait()
 
     def norm_block(b, out):
         outs_s[b] = out
@@ -478,8 +502,11 @@
     ring_arrived(3)
     ring_start(4)
 
-    fresh = [None, None] + [plan_ref[FLAGS + b].astype(F32) for b in range(2)]
-    later = [None, None] + [plan_ref[FLAGS + 2 + b].astype(F32) for b in range(2)]
+    own = [response_ref[3 * me + j] for j in range(3)]
+    fresh, later = [None, None], [None, None]
+    for j in (1, 2):
+        fresh.append(jnp.where(own[j] != own[j - 1], 1.0, 0.0).astype(F32))
+        later.append(jnp.where((own[j] >> 1) != (own[0] >> 1), 1.0, 0.0).astype(F32))
 
     state = None
     for b in (1, 2, 3):
@@ -545,9 +572,11 @@
                 sums_piece(hop, to_right), sum_recv.at[2 * (hop - 1) + (0 if to_right else 1)]
             )
 
+    loads[7].wait()
     sums_start(1)
 
     ring_arrived(4)
+    loads[6].wait()
 
     def cot_slots():
         yield cot_ref, head
@@ -592,7 +621,7 @@
             begun[0] += grad_in
     for slot in range(2):
         for piece in range(CHIPS):
-            grad_src[2 * piece + slot] = begun[slot][
+            grad_src[32 * piece + 16 * slot : 32 * piece + 16 * slot + 16, :] = begun[slot][
                 16 * (piece % 8) : 16 * (piece % 8) + 16,
                 128 * (piece // 8) : 128 * (piece // 8) + 128,
             ].astype(BF16)
@@ -600,8 +629,8 @@
     def send_grads(offset, carry):
         to = (me + offset) % N_SEQ
         send(
-            grad_src.at[pl.ds(2 * (to // 2), 2)],
-            grad_pieces.at[pl.ds(2 * (offset - 1), 2)],
+            grad_src.at[rows_of(to // 2, 32)],
+            grad_pieces.at[rows_of(offset - 1, 32)],
             seq_send.at[2],
             seq_recv.at[2],
             {"seq": to},
@@ -609,8 +638,7 @@
         return carry
 
     lax.fori_loop(1, N_SEQ, send_grads, 0)
-    for slot in range(2):
-        grad_pieces[62 + slot] = grad_src[2 * chip + slot]
+    grad_pieces[992:1024, :] = grad_src[rows_of(chip, 32), :]
 
     sums_arrived(1)
     sums_start(2)
@@ -629,15 +657,11 @@
         {"seq": 2 * chip + 1 - core},
     )
 
-    await_bytes(grad_pieces.at[pl.ds(0, 62)], seq_recv.at[2])
-
-    def owned_piece(offset):
-        one = grad_pieces[plan_ref[BACK + 2 * offset]].astype(F32)
-        two = grad_pieces[plan_ref[BACK + 2 * offset + 1]].astype(F32)
-        return (one + plan_ref[APART + offset].astype(F32) * two).astype(BF16)
+    await_bytes(grad_pieces.at[pl.ds(0, 992)], seq_recv.at[2])
+
+    owned_src[...] = dot(gather_s[...], grad_pieces[...]).astype(BF16)
 
     def send_owned(offset, carry):
-        owned_src[rows_of(offset - 1, 16), :] = owned_piece(offset)
         send(
             owned_src.at[rows_of(offset - 1, 16)],
             owned.at[rows_of(offset - 1, 16)],
@@ -648,7 +672,7 @@
         return carry
 
     lax.fori_loop(1, CHIPS, send_owned, 0)
-    owned[240:256, :] = owned_piece(0)
+    owned[240:256, :] = owned_src[240:256, :]
 
     await_bytes(weight_pair, seq_recv.at[4])
     for part in range(4):
@@ -690,8 +714,12 @@
             grad_state,
             state_in,
         )
-        grad_query_ref[SPAN * b : SPAN * b + SPAN, :] = found[0]
-        grad_key_ref[SPAN * b : SPAN * b + SPAN, :] = found[1]
+        for raw_ref, out_ref, grad, scale in (
+            (query_ref, grad_query_ref, found[0], SCALE),
+            (key_ref, grad_key_ref, found[1], 1.0),
+        ):
+            raw = raw_ref[SPAN * b : SPAN * b + SPAN, :].astype(F32)
+            out_ref[SPAN * b : SPAN * b + SPAN, :] = unit_back(raw, grad, scale)
         grad_value_ref[SPAN * b : SPAN * b + SPAN, :] = side_heads(found[2])
         grad_rates[b], grad_cums[b], grad_rows[b] = found[3:]
 
@@ -728,24 +756,32 @@
             index = 2 * (hop - 1) + (0 if to_right else 1)
             await_bytes(ring_piece(hop, to_right), ring_send.at[index])
             await_bytes(sums_piece(hop, to_right), sum_send.at[index])
-    await_bytes(pieces.at[pl.ds(0, 31)], seq_send.at[0])
+    await_bytes(pieces.at[pl.ds(0, 496)], seq_send.at[0])
     await_bytes(chosen.at[pl.ds(0, 480)], seq_send.at[1])
-    await_bytes(grad_pieces.at[pl.ds(0, 62)], seq_send.at[2])
+    await_bytes(grad_pieces.at[pl.ds(0, 992)], seq_send.at[2])
     await_bytes(owned.at[pl.ds(0, 240)], seq_send.at[3])
     await_bytes(weight_pair, seq_send.at[4])
     await_bytes(weight_in.at[pl.ds(0, 15 * 64)], seq_send.at[5])
 
 
 SCRATCH = [
+    pltpu.VMEM((256, 128), BF16),
+    pltpu.VMEM((256, 128), BF16),
+    pltpu.VMEM((256, 256), BF16),
+    pltpu.VMEM((256, 256), BF16),
+    pltpu.VMEM((2, 256), F32),
+    pltpu.VMEM((2, 256), F32),
+    pltpu.VMEM((2048, 256), BF16),
+    pltpu.VMEM((256, 256), BF16),
     pltpu.VMEM((7, 256, 256), BF16),
     pltpu.VMEM((256, 128), BF16),
-    pltpu.VMEM((32, 16, 128), BF16),
-    pltpu.VMEM((480, 128), BF16),
+    pltpu.VMEM((512, 128), BF16),
+    pltpu.VMEM((512, 128), BF16),
     pltpu.VMEM((512, 128), BF16),
     pltpu.VMEM((2, 128, 256), F32),
-    pltpu.VMEM((32, 16, 128), BF16),
-    pltpu.VMEM((64, 16, 128), BF16),
-    pltpu.VMEM((240, 128), BF16),
+    pltpu.VMEM((512, 128), BF16),
+    pltpu.VMEM((1024, 128), BF16),
+    pltpu.VMEM((256, 128), BF16),
     pltpu.VMEM((256, 128), BF16),
     pltpu.VMEM((8, 256, 256), BF16),
     pltpu.VMEM((8, 256, 256), BF16),
@@ -766,6 +802,9 @@
     pltpu.VMEM((3, 128, 128), F32),
     pltpu.VMEM((3, 128, 128), F32),
     pltpu.VMEM((256, 256), BF16),
+    pltpu.VMEM((512, 512), BF16),
+    pltpu.VMEM((256, 1024), BF16),
+    pltpu.SemaphoreType.DMA((8,)),
     pltpu.SemaphoreType.DMA((8,)),
     pltpu.SemaphoreType.DMA((8,)),
     pltpu.SemaphoreType.DMA((8,)),
@@ -775,24 +814,14 @@
 ]
 
 
-def unit_back(raw, grad, scale):
-    inv = unit_scale(raw)
-    unit = raw * inv
-    return (scale * inv) * (grad - unit * jnp.sum(grad * unit, axis=-1, keepdims=True))
-
-
-def finish_kernel(
-    query_ref, key_ref, layer, query, key, value, gate, rate, decay, weight,
-    layer_out, query_out, key_out, value_out, gate_out, rate_out, decay_out, weight_out,
-):
-    layer_out[...] = layer[...]
-    query_out[...] = unit_back(query_ref[...].astype(F32), query[...], SCALE)
-    key_out[...] = unit_back(key_ref[...].astype(F32), key[...], 1.0)
-    value_out[...] = value[...]
-    gate_out[...] = gate[...]
-    rate_out[...] = rate[...]
-    decay_out[...] = decay[...]
-    weight_out[...] = weight[...]
+def finish_kernel(*refs):
+    copies = [
+        pltpu.make_async_copy(refs[index], refs[8 + index], refs[16].at[index]) for index in range(8)
+    ]
+    for copy in copies:
+        copy.start()
+    for copy in copies:
+        copy.wait()
 
 
 RESULTS = [
@@ -813,32 +842,27 @@
 ):
     vmem = pl.BlockSpec(memory_space=pltpu.VMEM)
     smem = pl.BlockSpec(memory_space=pltpu.SMEM)
-    plan = pl.pallas_call(
-        plan_kernel,
-        out_shape=jax.ShapeDtypeStruct((96,), jnp.int32),
-        in_specs=[smem] * 2,
-        out_specs=smem,
-        scratch_shapes=[pltpu.SMEM((64,), jnp.int32)],
-    )(block_response, prefix_owner)
+    whole = pl.BlockSpec(memory_space=pl.ANY)
     results = pl.pallas_call(
         layer_kernel,
         out_shape=RESULTS,
-        in_specs=[vmem] * 8 + [smem],
+        in_specs=[whole] * 8 + [smem] * 2,
         out_specs=[vmem] * 8,
         scratch_shapes=SCRATCH,
         compiler_params=pltpu.CompilerParams(
-            collective_id=0, has_side_effects=True, vmem_limit_bytes=48 * 1024 * 1024
+            collective_id=0, has_side_effects=True, vmem_limit_bytes=56 * 1024 * 1024
         ),
     )(
         query_rows, key_rows, value_rows, output_gate, write_rate, log_decay,
-        out_weight, out_cotangent, plan,
+        out_weight, out_cotangent, block_response, prefix_owner,
     )
     return pl.pallas_call(
         finish_kernel,
         out_shape=RESULTS,
-        in_specs=[vmem] * 10,
-        out_specs=[vmem] * 8,
-    )(query_rows, key_rows, *results)
+        in_specs=[whole] * 8,
+        out_specs=[whole] * 8,
+        scratch_shapes=[pltpu.SemaphoreType.DMA((8,))],
+    )(*results)
 
 
 def solution(mesh):

time: 66 us -> 81.4 us (1.23)
  Pallas kernels: 52.5 us -> 80.3 us
  local copies, waits for them, and re-layouts: 12.2 us -> 0 us
    pallas_call x3 -> x2, Pallas kernels: 52.5 us -> 80.3 us  [the longest x1 49.2 us: per_device(): pl.pallas_call(layer_kernel, out_shape=RESULTS, in_specs=[whole] * 8 + [s...]
    unnamed x34 -> x0, local copies, waits for them, and re-layouts: 12.2 us -> none
where the time goes in v2:
time: 81.4 us; the launch traced here: 80.9 us
  Pallas kernels  80.3 us (99%)
    pallas_call x1, Pallas kernels, per_device(): pl.pallas_call(layer_kernel, out_shape=RESULTS, in_specs=[whole] * 8 + [s...  49.2 us
    pallas_call x1, Pallas kernels, per_device(): pl.pallas_call(finish_kernel, out_shape=RESULTS, in_specs=[whole] * 8, ou...  31.1 us

profile of v2, /device:TPU:1, one launch (start us, length us, event | category | flops | bytes accessed | tf_op | source)
XLA Modules:
  0.0 80.9 jit_solution(4654062582272327197)
XLA Ops:
  0.6 49.2 %shard_map.161 = (bf16[256,256]{1,0:T(8,128)(2,1)}, f32[256,128]{1,0:T(8,128)}, f32[256,128]{1,0:T(8,128)}, f32[256,256]{1,0:T(8,128)}, f32[256,256]{1,0:T(8,128...) custom-call(bf16[256,128]{1,0:T(8,128)(2,1)} %query_hbm.1, bf16[256,128]{1,0:T(8,128)(2,1)} %key_hbm.1, ...), custom_call_target="tpu_custom_call" | custom-call | tf_op jit(solution)/shard_map/pallas_call | solution.py:846
  49.9 31.1 %shard_map.162 = (bf16[256,256]{1,0:T(8,128)(2,1)}, f32[256,128]{1,0:T(8,128)}, f32[256,128]{1,0:T(8,128)}, f32[256,256]{1,0:T(8,128)}, f32[256,256]{1,0:T(8,128...) custom-call(bf16[256,256]{1,0:T(8,128)(2,1)} %get-tuple-element.16.refs_0_, ...), custom_call_target="tpu_custom_call" | custom-call | tf_op jit(solution)/shard_map/pallas_call | solution.py:859

commit v3 on v2

--- a/solution.py
+++ b/solution.py
@@ -309,6 +309,7 @@
     key_state_s,
     query_state_s,
     normed_s,
+    share_s,
     pick_s,
     gather_s,
     load_sem,
@@ -353,36 +354,40 @@
     lax.fori_loop(1, N_SEQ, greet, 0)
     for neighbour in (left, right):
         pl.semaphore_signal(barrier, inc=1, device_id={"head": neighbour}, device_id_type=MESH)
-    pl.semaphore_wait(barrier, N_SEQ + 1)
-
-    def ring_piece(hop, to_right):
-        if hop == 4:
-            return cots.at[3, pl.ds(0 if to_right else 128, 128)]
-        return cots.at[hop - 1 if to_right else 3 + hop]
-
-    def ring_start(hop):
-        for to_right in (True, False):
-            if hop == 1:
-                src = cot_hbm
-            else:
-                src = cots.at[hop - 2 if to_right else 2 + hop]
-                if hop == 4:
-                    src = src.at[pl.ds(0 if to_right else 128, 128)]
-            index = 2 * (hop - 1) + (0 if to_right else 1)
-            send(
-                src,
-                ring_piece(hop, to_right),
-                ring_send.at[index],
-                ring_recv.at[index],
-                {"head": right if to_right else left},
-            )
-
-    def ring_arrived(hop):
-        for to_right in (True, False):
-            index = 2 * (hop - 1) + (0 if to_right else 1)
-            await_bytes(ring_piece(hop, to_right), ring_recv.at[index])
-
-    ring_start(1)
+
+    def ring_order(hop, to_right):
+        order = (0, 1, 2, 3) if to_right else (2, 3, 0, 1)
+        return order[:2] if hop == 4 else order
+
+    def ring_chunk(hop, to_right, chunk):
+        slot = hop - 1 if to_right or hop == 4 else 3 + hop
+        return cots.at[slot, pl.ds(64 * chunk, 64)]
+
+    def ring_index(hop, to_right, chunk):
+        return 8 * (hop - 1) + (0 if to_right else 4) + chunk
+
+    def ring_start(hop, to_right, chunk):
+        if hop == 1:
+            src = cot_hbm.at[pl.ds(64 * chunk, 64)]
+        else:
+            src = ring_chunk(hop - 1, to_right, chunk)
+        send(
+            src,
+            ring_chunk(hop, to_right, chunk),
+            ring_send.at[0],
+            ring_recv.at[ring_index(hop, to_right, chunk)],
+            {"head": right if to_right else left},
+        )
+
+    def ring_relay(hop):
+        for place in range(2 if hop == 4 else 4):
+            for to_right in (True, False):
+                chunk = ring_order(hop, to_right)[place]
+                await_bytes(
+                    ring_chunk(hop, to_right, chunk), ring_recv.at[ring_index(hop, to_right, chunk)]
+                )
+                if hop < 4 and chunk in ring_order(hop + 1, to_right):
+                    ring_start(hop + 1, to_right, chunk)
 
     for load in loads[:5]:
         load.wait()
@@ -410,7 +415,12 @@
     def tail_of(b):
         return twice(keys[b]) * cols[b][4]
 
-    inverse_s[0] = inverse([tables_of(0)])[0].astype(BF16)
+    first_system = tables_of(0)
+    pl.semaphore_wait(barrier, N_SEQ + 1)
+    for place in range(4):
+        for to_right in (True, False):
+            ring_start(1, to_right, ring_order(1, to_right)[place])
+    inverse_s[0] = inverse([first_system])[0].astype(BF16)
     update = dot(inverse_s[0], cols[0][2] * block_of(value_ref, 0))
     update_s[0] = update
     final = dot(tail_of(0), diagonal_heads(update), "tn")
@@ -430,11 +440,6 @@
 
     lax.fori_loop(1, N_SEQ, send_pieces, 0)
     pieces[496:512, :] = piece_src[rows_of(chip, 16), :]
-
-    ring_arrived(1)
-    ring_start(2)
-    for b, found in zip((1, 2, 3), inverse([tables_of(b) for b in (1, 2, 3)])):
-        inverse_s[b] = found.astype(BF16)
 
     def owner_of(device, slot):
         prompt = (response_ref[3 * device] >> 1) + slot
@@ -463,6 +468,12 @@
         here = (owner == target) & ((row & 15) == (col & 15))
         gather_s[:, 128 * quarter : 128 * quarter + 128] = jnp.where(here, 1.0, 0.0).astype(BF16)
 
+    systems = [tables_of(b) for b in (1, 2, 3)]
+    ring_relay(1)
+    for b, found in zip((1, 2, 3), inverse(systems)):
+        inverse_s[b] = found.astype(BF16)
+    ring_relay(2)
+
     await_bytes(pieces.at[pl.ds(0, 496)], seq_recv.at[0])
 
     chosen_src[...] = dot(pick_s[...], pieces[...]).astype(BF16)
@@ -480,9 +491,6 @@
     lax.fori_loop(1, CHIPS, send_chosen, 0)
     chosen[480:512, :] = chosen_src[480:512, :]
 
-    ring_arrived(2)
-    ring_start(3)
-
     loads[5].wait()
 
     def norm_block(b, out):
@@ -491,6 +499,7 @@
         normed_s[SPAN * b : SPAN * b + SPAN, :] = result
 
     norm_block(0, dot3(scores_s[0], update_s[0]))
+    ring_relay(3)
 
     await_bytes(chosen.at[pl.ds(0, 480)], seq_recv.at[1])
     for slot in range(2):
@@ -499,9 +508,6 @@
             starts[slot, 16 * (piece % 8) : 16 * (piece % 8) + 16, 128 * (piece // 8) : 128 * (piece // 8) + 128] = (
                 chosen[pl.ds(pl.multiple_of(place * 32 + 16 * slot, 16), 16), :].astype(F32)
             )
-    ring_arrived(3)
-    ring_start(4)
-
     own = [response_ref[3 * me + j] for j in range(3)]
     fresh, later = [None, None], [None, None]
     for j in (1, 2):
@@ -531,51 +537,68 @@
         block = (head + distance + N_HEAD) % N_HEAD
         return dot(normed_s[...], weight_ref[rows_of(block, 256), :], "nt")
 
-    def sums_start(hop):
+    def sums_order(hop, to_right):
+        if hop == 1:
+            return (0, 1) if to_right else (2, 3)
+        return (2, 3, 0, 1) if to_right else (0, 1, 2, 3)
+
+    def sums_slot(hop, to_right):
+        return 2 * (hop - 1) + (0 if to_right else 1)
+
+    def sums_start(hop, to_right, chunk):
+        here = (sums_slot(hop, to_right), pl.ds(64 * chunk, 64))
+        send(
+            sums_src.at[here],
+            sums.at[here],
+            sum_send.at[0],
+            sum_recv.at[ring_index(hop, to_right, chunk)],
+            {"head": right if to_right else left},
+        )
+
+    def sums_prepare(hop):
         for to_right in (True, False):
-            index = 2 * (hop - 1) + (0 if to_right else 1)
-            if hop == 1:
-                half = pl.ds(0 if to_right else 128, 128)
-                block = (head + 4) % N_HEAD
-                sums_src[index, half, :] = dot(
-                    normed_s[half, :], weight_ref[rows_of(block, 256), :], "nt"
-                ).astype(BF16)
-                src, dst = sums_src.at[index, half], sums.at[index, half]
-            else:
-                total = share(5 - hop if to_right else hop - 5)
-                if hop == 2:
-                    low = 0 if to_right else 128
-                    sums_src[index] = total.astype(BF16)
-                    sums_src[index, low : low + 128, :] = (
-                        total[low : low + 128] + sums[index - 2, low : low + 128, :].astype(F32)
+            share_s[sums_slot(hop, to_right)] = share(5 - hop if to_right else hop - 5)
+
+    def sums_begin():
+        across = share(4)
+        for to_right in (True, False):
+            low = 0 if to_right else 128
+            sums_src[sums_slot(1, to_right), low : low + 128, :] = across[low : low + 128].astype(BF16)
+        for place in range(2):
+            for to_right in (True, False):
+                sums_start(1, to_right, sums_order(1, to_right)[place])
+        sums_prepare(2)
+        for to_right in (True, False):
+            slot, low = sums_slot(2, to_right), 128 if to_right else 0
+            sums_src[slot, low : low + 128, :] = share_s[slot, low : low + 128, :].astype(BF16)
+        for place in range(2):
+            for to_right in (True, False):
+                sums_start(2, to_right, sums_order(2, to_right)[place])
+
+    def sums_await(hop, to_right, chunk):
+        here = (sums_slot(hop, to_right), pl.ds(64 * chunk, 64))
+        await_bytes(sums.at[here], sum_recv.at[ring_index(hop, to_right, chunk)])
+
+    def sums_relay(hop):
+        for place in range(2 if hop == 1 else 4):
+            for to_right in (True, False):
+                chunk = sums_order(hop, to_right)[place]
+                sums_await(hop, to_right, chunk)
+                if hop < 4:
+                    here = slice(64 * chunk, 64 * chunk + 64)
+                    slot = sums_slot(hop + 1, to_right)
+                    sums_src[slot, here, :] = (
+                        share_s[slot, here, :]
+                        + sums[sums_slot(hop, to_right), here, :].astype(F32)
                     ).astype(BF16)
-                else:
-                    sums_src[index] = (total + sums[index - 2].astype(F32)).astype(BF16)
-                src, dst = sums_src.at[index], sums.at[index]
-            send(
-                src,
-                dst,
-                sum_send.at[index],
-                sum_recv.at[index],
-                {"head": right if to_right else left},
-            )
-
-    def sums_piece(hop, to_right):
-        index = 2 * (hop - 1) + (0 if to_right else 1)
-        if hop == 1:
-            return sums.at[index, pl.ds(0 if to_right else 128, 128)]
-        return sums.at[index]
-
-    def sums_arrived(hop):
-        for to_right in (True, False):
-            await_bytes(
-                sums_piece(hop, to_right), sum_recv.at[2 * (hop - 1) + (0 if to_right else 1)]
-            )
+                    sums_start(hop + 1, to_right, chunk)
+        if hop < 3:
+            sums_prepare(hop + 2)
 
     loads[7].wait()
-    sums_start(1)
-
-    ring_arrived(4)
+    sums_begin()
+
+    ring_relay(4)
     loads[6].wait()
 
     def cot_slots():
@@ -640,8 +663,7 @@
     lax.fori_loop(1, N_SEQ, send_grads, 0)
     grad_pieces[992:1024, :] = grad_src[rows_of(chip, 32), :]
 
-    sums_arrived(1)
-    sums_start(2)
+    sums_relay(1)
     for slot_ref, block in cot_slots():
         share_w = dot(slot_ref[...], normed_s[...], "tn").astype(BF16)
         for quarter in range(4):
@@ -657,6 +679,8 @@
         {"seq": 2 * chip + 1 - core},
     )
 
+    sums_relay(2)
+
     await_bytes(grad_pieces.at[pl.ds(0, 992)], seq_recv.at[2])
 
     owned_src[...] = dot(gather_s[...], grad_pieces[...]).astype(BF16)
@@ -694,8 +718,6 @@
         return carry
 
     lax.fori_loop(1, CHIPS, send_weight, 0)
-    sums_arrived(2)
-    sums_start(3)
 
     grad_cums, grad_rates, grad_rows = [None] * 4, [None] * 4, [None] * 4
 
@@ -725,9 +747,8 @@
 
     for b in (1, 2, 3):
         finish_block(b, grad_state_s[b], (state_s[b - 1], key_state_s[b - 1], query_state_s[b - 1]))
-        if b == 2:
-            sums_arrived(3)
-            sums_start(4)
+        if b == 1:
+            sums_relay(3)
 
     await_bytes(owned.at[pl.ds(0, 240)], seq_recv.at[3])
     for piece in range(CHIPS):
@@ -748,14 +769,11 @@
         total += weight_in[64 * slot : 64 * slot + 64, :].astype(F32)
     grad_weight_ref[...] = total
     total = share(0)
-    sums_arrived(4)
+    sums_relay(4)
     layer_ref[...] = (total + sums[6].astype(F32) + sums[7].astype(F32)).astype(BF16)
 
-    for hop in (1, 2, 3, 4):
-        for to_right in (True, False):
-            index = 2 * (hop - 1) + (0 if to_right else 1)
-            await_bytes(ring_piece(hop, to_right), ring_send.at[index])
-            await_bytes(sums_piece(hop, to_right), sum_send.at[index])
+    await_bytes(cots, ring_send.at[0])
+    await_bytes(sums.at[pl.ds(0, 7)], sum_send.at[0])
     await_bytes(pieces.at[pl.ds(0, 496)], seq_send.at[0])
     await_bytes(chosen.at[pl.ds(0, 480)], seq_send.at[1])
     await_bytes(grad_pieces.at[pl.ds(0, 992)], seq_send.at[2])
@@ -802,26 +820,22 @@
     pltpu.VMEM((3, 128, 128), F32),
     pltpu.VMEM((3, 128, 128), F32),
     pltpu.VMEM((256, 256), BF16),
+    pltpu.VMEM((8, 256, 256), F32),
     pltpu.VMEM((512, 512), BF16),
     pltpu.VMEM((256, 1024), BF16),
     pltpu.SemaphoreType.DMA((8,)),
-    pltpu.SemaphoreType.DMA((8,)),
-    pltpu.SemaphoreType.DMA((8,)),
-    pltpu.SemaphoreType.DMA((8,)),
-    pltpu.SemaphoreType.DMA((8,)),
+    pltpu.SemaphoreType.DMA((1,)),
+    pltpu.SemaphoreType.DMA((32,)),
+    pltpu.SemaphoreType.DMA((1,)),
+    pltpu.SemaphoreType.DMA((32,)),
     pltpu.SemaphoreType.DMA((6,)),
     pltpu.SemaphoreType.DMA((6,)),
 ]
 
 
 def finish_kernel(*refs):
-    copies = [
-        pltpu.make_async_copy(refs[index], refs[8 + index], refs[16].at[index]) for index in range(8)
-    ]
-    for copy in copies:
-        copy.start()
-    for copy in copies:
-        copy.wait()
+    for index in range(8):
+        refs[8 + index][...] = refs[index][...]
 
 
 RESULTS = [
@@ -859,9 +873,8 @@
     return pl.pallas_call(
         finish_kernel,
         out_shape=RESULTS,
-        in_specs=[whole] * 8,
-        out_specs=[whole] * 8,
-        scratch_shapes=[pltpu.SemaphoreType.DMA((8,))],
+        in_specs=[vmem] * 8,
+        out_specs=[vmem] * 8,
     )(*results)
 
 

time: 81.4 us -> 51.4 us (0.63)
  Pallas kernels: 80.3 us -> 50.6 us
    pallas_call x1, Pallas kernels: 31.1 us -> 2.17 us  [per_device(): pl.pallas_call(finish_kernel, out_shape=RESULTS, in_specs=[vmem] * 8, out...]
where the time goes in v3:
time: 51.4 us; the launch traced here: 51.2 us
  Pallas kernels  50.6 us (98%)
  between operations  0.64 us (1%)
    pallas_call x1, Pallas kernels, per_device(): pl.pallas_call(layer_kernel, out_shape=RESULTS, in_specs=[whole] * 8 + [s...  48.4 us
    pallas_call x1, Pallas kernels, per_device(): pl.pallas_call(finish_kernel, out_shape=RESULTS, in_specs=[vmem] * 8, out...  2.17 us

profile of v3, /device:TPU:1, one launch (start us, length us, event | category | flops | bytes accessed | tf_op | source)
XLA Modules:
  0.0 51.2 jit_solution(16677634064356561262)
XLA Ops:
  0.6 48.4 %shard_map.161 = (bf16[256,256]{1,0:T(8,128)(2,1)}, f32[256,128]{1,0:T(8,128)}, f32[256,128]{1,0:T(8,128)}, f32[256,256]{1,0:T(8,128)}, f32[256,256]{1,0:T(8,128...) custom-call(bf16[256,128]{1,0:T(8,128)(2,1)} %query_hbm.1, bf16[256,128]{1,0:T(8,128)(2,1)} %key_hbm.1, ...), custom_call_target="tpu_custom_call" | custom-call | tf_op jit(solution)/shard_map/pallas_call | solution.py:860
  49.1 2.2 %shard_map.162 = (bf16[256,256]{1,0:T(8,128)(2,1)}, f32[256,128]{1,0:T(8,128)}, f32[256,128]{1,0:T(8,128)}, f32[256,256]{1,0:T(8,128)}, f32[256,256]{1,0:T(8,128...) custom-call(bf16[256,256]{1,0:T(8,128)(2,1)} %get-tuple-element.16.refs_0_, ...), custom_call_target="tpu_custom_call" | custom-call | tf_op jit(solution)/shard_map/pallas_call | solution.py:873

commit v4 on v3

--- a/solution.py
+++ b/solution.py
@@ -146,7 +146,7 @@
     return within, system, query_key
 
 
-def inverse(systems):
+def inverse(systems, between=None):
     row, col = iotas()
     found = None
     for level in range(6):
@@ -158,6 +158,8 @@
         else:
             half = [dot3(one, two) for one, two in zip(found, below)]
             found = [one - dot3(two, one) for one, two in zip(found, half)]
+            if between is not None:
+                between(level)
     return found
 
 
@@ -379,8 +381,11 @@
             {"head": right if to_right else left},
         )
 
-    def ring_relay(hop):
-        for place in range(2 if hop == 4 else 4):
+    ring_steps = [(hop, place) for hop in (1, 2, 3, 4) for place in range(2 if hop == 4 else 4)]
+
+    def ring_pump(count):
+        for _ in range(count):
+            hop, place = ring_steps.pop(0)
             for to_right in (True, False):
                 chunk = ring_order(hop, to_right)[place]
                 await_bytes(
@@ -446,33 +451,20 @@
         found = owner_ref[jnp.minimum(prompt, N_SEQ - 1)]
         return jnp.where(prompt < N_SEQ, found, -1)
 
-    row, col = iotas((32, 512))
+    row, _ = iotas((32, 1))
+    _, col = iotas((1, 512))
     source = (me + 31 - (col >> 4)) % N_SEQ
+    same_row = (row & 15) == (col & 15)
     for place in range(CHIPS):
         to = 2 * ((chip + place + 1) % CHIPS) + core
         wanted = jnp.where(row < 16, owner_of(to, 0), owner_of(to, 1))
-        here = (source == wanted) & ((row & 15) == (col & 15))
+        here = (source == wanted) & same_row
         pick_s[32 * place : 32 * place + 32, :] = jnp.where(here, 1.0, 0.0).astype(BF16)
 
-    for quarter in range(8):
-        columns_here = []
-        for place in range(4 * quarter, 4 * quarter + 4):
-            device = (me + 31 - place) % N_SEQ
-            columns_here.append((owner_of(device, 0), owner_of(device, 1)))
-        row, col = iotas((256, 128))
-        owner = jnp.full((256, 128), -1, jnp.int32)
-        for index, (one, two) in enumerate(columns_here):
-            owner = jnp.where((col >> 4) == 2 * index, one, owner)
-            owner = jnp.where((col >> 4) == 2 * index + 1, two, owner)
-        target = 2 * ((chip + 1 + (row >> 4)) % CHIPS) + core
-        here = (owner == target) & ((row & 15) == (col & 15))
-        gather_s[:, 128 * quarter : 128 * quarter + 128] = jnp.where(here, 1.0, 0.0).astype(BF16)
-
-    systems = [tables_of(b) for b in (1, 2, 3)]
-    ring_relay(1)
-    for b, found in zip((1, 2, 3), inverse(systems)):
-        inverse_s[b] = found.astype(BF16)
-    ring_relay(2)
+    systems = []
+    for b in (1, 2, 3):
+        systems.append(tables_of(b))
+        ring_pump(2 if b == 3 else 1)
 
     await_bytes(pieces.at[pl.ds(0, 496)], seq_recv.at[0])
 
@@ -491,6 +483,12 @@
     lax.fori_loop(1, CHIPS, send_chosen, 0)
     chosen[480:512, :] = chosen_src[480:512, :]
 
+    def between(level):
+        if level < 5:
+            ring_pump(1)
+
+    for b, found in zip((1, 2, 3), inverse(systems, between)):
+        inverse_s[b] = found.astype(BF16)
     loads[5].wait()
 
     def norm_block(b, out):
@@ -499,7 +497,7 @@
         normed_s[SPAN * b : SPAN * b + SPAN, :] = result
 
     norm_block(0, dot3(scores_s[0], update_s[0]))
-    ring_relay(3)
+    ring_pump(2)
 
     await_bytes(chosen.at[pl.ds(0, 480)], seq_recv.at[1])
     for slot in range(2):
@@ -532,6 +530,8 @@
         if b < 3:
             state = last_growth(rows, b) * state + dot(tail_of(b), diagonal_heads(update), "tn")
         norm_block(b, growth * query_state + dot3(scores_s[b], update))
+        if b < 3:
+            ring_pump(1)
 
     def share(distance):
         block = (head + distance + N_HEAD) % N_HEAD
@@ -575,41 +575,39 @@
             for to_right in (True, False):
                 sums_start(2, to_right, sums_order(2, to_right)[place])
 
-    def sums_await(hop, to_right, chunk):
-        here = (sums_slot(hop, to_right), pl.ds(64 * chunk, 64))
-        await_bytes(sums.at[here], sum_recv.at[ring_index(hop, to_right, chunk)])
-
-    def sums_relay(hop):
-        for place in range(2 if hop == 1 else 4):
+    sums_steps = [(hop, place) for hop in (1, 2, 3, 4) for place in range(2 if hop == 1 else 4)]
+
+    def sums_pump(count):
+        for _ in range(count):
+            hop, place = sums_steps.pop(0)
             for to_right in (True, False):
                 chunk = sums_order(hop, to_right)[place]
-                sums_await(hop, to_right, chunk)
+                here = pl.ds(64 * chunk, 64)
+                arrived = sums.at[sums_slot(hop, to_right), here]
+                await_bytes(arrived, sum_recv.at[ring_index(hop, to_right, chunk)])
                 if hop < 4:
-                    here = slice(64 * chunk, 64 * chunk + 64)
                     slot = sums_slot(hop + 1, to_right)
                     sums_src[slot, here, :] = (
-                        share_s[slot, here, :]
-                        + sums[sums_slot(hop, to_right), here, :].astype(F32)
+                        share_s[slot, here, :] + arrived[...].astype(F32)
                     ).astype(BF16)
                     sums_start(hop + 1, to_right, chunk)
-        if hop < 3:
-            sums_prepare(hop + 2)
 
     loads[7].wait()
     sums_begin()
 
-    ring_relay(4)
     loads[6].wait()
 
     def cot_slots():
         yield cot_ref, head
-        for hop in (1, 2, 3, 4):
+        for hop in (1, 2, 3):
             yield cots.at[hop - 1], (head - hop + N_HEAD) % N_HEAD
-        for hop in (1, 2, 3):
             yield cots.at[3 + hop], (head + hop) % N_HEAD
+        yield cots.at[3], (head + 4) % N_HEAD
 
     grad_normed = None
-    for slot_ref, block in cot_slots():
+    for index, (slot_ref, block) in enumerate(cot_slots()):
+        if index == 7:
+            ring_pump(2)
         term = dot(slot_ref[...], weight_ref[rows_of(block, 256), :])
         grad_normed = term if grad_normed is None else grad_normed + term
     for b in range(4):
@@ -640,6 +638,8 @@
             begun[0] += (fresh[b] * (1.0 - later[b])) * grad_in
             begun[1] += (fresh[b] * later[b]) * grad_in
             grad_state = (1.0 - fresh[b]) * grad_in
+            if b == 2:
+                sums_pump(1)
         else:
             begun[0] += grad_in
     for slot in range(2):
@@ -663,14 +663,18 @@
     lax.fori_loop(1, N_SEQ, send_grads, 0)
     grad_pieces[992:1024, :] = grad_src[rows_of(chip, 32), :]
 
-    sums_relay(1)
-    for slot_ref, block in cot_slots():
+    sums_prepare(3)
+    sums_pump(1)
+
+    for index, (slot_ref, block) in enumerate(cot_slots()):
         share_w = dot(slot_ref[...], normed_s[...], "tn").astype(BF16)
         for quarter in range(4):
             place = (quarter % 2) * 1024 + (2 * block + quarter // 2) * 64
             weight_src[pl.ds(pl.multiple_of(place, 64), 64), :] = share_w[
                 64 * quarter : 64 * quarter + 64
             ]
+        if index % 2 == 1:
+            sums_pump(1)
     send(
         weight_src.at[rows_of(1 - core, 1024)],
         weight_pair,
@@ -679,7 +683,19 @@
         {"seq": 2 * chip + 1 - core},
     )
 
-    sums_relay(2)
+    sums_prepare(4)
+    _, col = iotas((1, 128))
+    row, _ = iotas((256, 1))
+    target = 2 * ((chip + 1 + (row >> 4)) % CHIPS) + core
+    for part in range(8):
+        owner = jnp.full((1, 128), -1, jnp.int32)
+        for index in range(4):
+            device = (me + 31 - (4 * part + index)) % N_SEQ
+            for slot in range(2):
+                owner = jnp.where((col >> 4) == 2 * index + slot, owner_of(device, slot), owner)
+        here = (owner == target) & ((row & 15) == (col & 15))
+        gather_s[:, 128 * part : 128 * part + 128] = jnp.where(here, 1.0, 0.0).astype(BF16)
+    sums_pump(1)
 
     await_bytes(grad_pieces.at[pl.ds(0, 992)], seq_recv.at[2])
 
@@ -696,6 +712,7 @@
         return carry
 
     lax.fori_loop(1, CHIPS, send_owned, 0)
+    sums_pump(1)
     owned[240:256, :] = owned_src[240:256, :]
 
     await_bytes(weight_pair, seq_recv.at[4])
@@ -747,9 +764,10 @@
 
     for b in (1, 2, 3):
         finish_block(b, grad_state_s[b], (state_s[b - 1], key_state_s[b - 1], query_state_s[b - 1]))
-        if b == 1:
-            sums_relay(3)
-
+        if b < 3:
+            sums_pump(1)
+
+    share_s[0] = share(0)
     await_bytes(owned.at[pl.ds(0, 240)], seq_recv.at[3])
     for piece in range(CHIPS):
         place = (chip - piece + 15) % CHIPS
@@ -768,9 +786,8 @@
     for slot in range(15):
         total += weight_in[64 * slot : 64 * slot + 64, :].astype(F32)
     grad_weight_ref[...] = total
-    total = share(0)
-    sums_relay(4)
-    layer_ref[...] = (total + sums[6].astype(F32) + sums[7].astype(F32)).astype(BF16)
+    sums_pump(4)
+    layer_ref[...] = (share_s[0] + sums[6].astype(F32) + sums[7].astype(F32)).astype(BF16)
 
     await_bytes(cots, ring_send.at[0])
     await_bytes(sums.at[pl.ds(0, 7)], sum_send.at[0])

time: 51.4 us -> 51.1 us (level)
  no operation moved by 1% of the time
where the time goes in v4:
time: 51.1 us; the launch traced here: 51 us
  Pallas kernels  50.4 us (99%)
  between operations  0.64 us (1%)
    pallas_call x1, Pallas kernels, per_device(): pl.pallas_call(layer_kernel, out_shape=RESULTS, in_specs=[whole] * 8 + [s...  48.2 us
    pallas_call x1, Pallas kernels, per_device(): pl.pallas_call(finish_kernel, out_shape=RESULTS, in_specs=[vmem] * 8, out...  2.17 us

profile of v4, /device:TPU:1, one launch (start us, length us, event | category | flops | bytes accessed | tf_op | source)
XLA Modules:
  0.0 51.0 jit_solution(7799156023696010296)
XLA Ops:
  0.6 48.2 %shard_map.161 = (bf16[256,256]{1,0:T(8,128)(2,1)}, f32[256,128]{1,0:T(8,128)}, f32[256,128]{1,0:T(8,128)}, f32[256,256]{1,0:T(8,128)}, f32[256,256]{1,0:T(8,128...) custom-call(bf16[256,128]{1,0:T(8,128)(2,1)} %query_hbm.1, bf16[256,128]{1,0:T(8,128)(2,1)} %key_hbm.1, ...), custom_call_target="tpu_custom_call" | custom-call | tf_op jit(solution)/shard_map/pallas_call | solution.py:877
  48.8 2.2 %shard_map.162 = (bf16[256,256]{1,0:T(8,128)(2,1)}, f32[256,128]{1,0:T(8,128)}, f32[256,128]{1,0:T(8,128)}, f32[256,256]{1,0:T(8,128)}, f32[256,256]{1,0:T(8,128...) custom-call(bf16[256,256]{1,0:T(8,128)(2,1)} %get-tuple-element.16.refs_0_, ...), custom_call_target="tpu_custom_call" | custom-call | tf_op jit(solution)/shard_map/pallas_call | solution.py:890

commit v5 on v4

--- a/solution.py
+++ b/solution.py
@@ -312,6 +312,7 @@
     query_state_s,
     normed_s,
     share_s,
+    turned_s,
     pick_s,
     gather_s,
     load_sem,
@@ -324,8 +325,8 @@
 ):
     me = lax.axis_index("seq")
     head = lax.axis_index("head")
-    chip, core = me // 2, me % 2
-    right, left = (head + 1) % N_HEAD, (head + N_HEAD - 1) % N_HEAD
+    chip, core = lax.div(me, 2), lax.rem(me, 2)
+    right, left = lax.rem(head + 1, N_HEAD), lax.rem(head + N_HEAD - 1, N_HEAD)
 
     loads = [
         pltpu.make_async_copy(src, dst, load_sem.at[index])
@@ -349,7 +350,7 @@
 
     def greet(offset, carry):
         pl.semaphore_signal(
-            barrier, inc=1, device_id={"seq": (me + offset) % N_SEQ}, device_id_type=MESH
+            barrier, inc=1, device_id={"seq": lax.rem(me + offset, N_SEQ)}, device_id_type=MESH
         )
         return carry
 
@@ -394,6 +395,16 @@
                 if hop < 4 and chunk in ring_order(hop + 1, to_right):
                     ring_start(hop + 1, to_right, chunk)
 
+    def cot_slots():
+        yield cot_ref, head
+        for hop in (1, 2, 3):
+            yield cots.at[hop - 1], (head - hop + N_HEAD) % N_HEAD
+            yield cots.at[3 + hop], (head + hop) % N_HEAD
+        yield cots.at[3], (head + 4) % N_HEAD
+
+    def turn(index, slot_ref):
+        turned_s[index] = jnp.transpose(slot_ref[...])
+
     for load in loads[:5]:
         load.wait()
     rate2, decay2 = rate_ref[...], decay_ref[...]
@@ -433,9 +444,9 @@
     piece_src[128:256, :] = final[:, 128:].astype(BF16)
 
     def send_pieces(offset, carry):
-        to = (me + offset) % N_SEQ
+        to = lax.rem(me + offset, N_SEQ)
         send(
-            piece_src.at[rows_of(to // 2, 16)],
+            piece_src.at[rows_of(lax.div(to, 2), 16)],
             pieces.at[rows_of(offset - 1, 16)],
             seq_send.at[0],
             seq_recv.at[0],
@@ -456,7 +467,7 @@
     source = (me + 31 - (col >> 4)) % N_SEQ
     same_row = (row & 15) == (col & 15)
     for place in range(CHIPS):
-        to = 2 * ((chip + place + 1) % CHIPS) + core
+        to = 2 * lax.rem(chip + place + 1, CHIPS) + core
         wanted = jnp.where(row < 16, owner_of(to, 0), owner_of(to, 1))
         here = (source == wanted) & same_row
         pick_s[32 * place : 32 * place + 32, :] = jnp.where(here, 1.0, 0.0).astype(BF16)
@@ -476,7 +487,7 @@
             chosen.at[rows_of(offset - 1, 32)],
             seq_send.at[1],
             seq_recv.at[1],
-            {"seq": 2 * ((chip + offset) % CHIPS) + core},
+            {"seq": 2 * lax.rem(chip + offset, CHIPS) + core},
         )
         return carry
 
@@ -497,12 +508,16 @@
         normed_s[SPAN * b : SPAN * b + SPAN, :] = result
 
     norm_block(0, dot3(scores_s[0], update_s[0]))
+    loads[6].wait()
+    for index, (slot_ref, _) in enumerate(cot_slots()):
+        if index < 5:
+            turn(index, slot_ref)
     ring_pump(2)
 
     await_bytes(chosen.at[pl.ds(0, 480)], seq_recv.at[1])
     for slot in range(2):
         for piece in range(CHIPS):
-            place = (chip - piece + 15) % CHIPS
+            place = lax.rem(chip + 15 - piece, CHIPS)
             starts[slot, 16 * (piece % 8) : 16 * (piece % 8) + 16, 128 * (piece // 8) : 128 * (piece // 8) + 128] = (
                 chosen[pl.ds(pl.multiple_of(place * 32 + 16 * slot, 16), 16), :].astype(F32)
             )
@@ -594,22 +609,30 @@
 
     loads[7].wait()
     sums_begin()
-
-    loads[6].wait()
-
-    def cot_slots():
-        yield cot_ref, head
-        for hop in (1, 2, 3):
-            yield cots.at[hop - 1], (head - hop + N_HEAD) % N_HEAD
-            yield cots.at[3 + hop], (head + hop) % N_HEAD
-        yield cots.at[3], (head + 4) % N_HEAD
+    for index, (slot_ref, _) in enumerate(cot_slots()):
+        if index in (5, 6):
+            turn(index, slot_ref)
 
     grad_normed = None
     for index, (slot_ref, block) in enumerate(cot_slots()):
         if index == 7:
             ring_pump(2)
+            turn(7, slot_ref)
         term = dot(slot_ref[...], weight_ref[rows_of(block, 256), :])
         grad_normed = term if grad_normed is None else grad_normed + term
+        share_w = dot(turned_s[index], normed_s[...]).astype(BF16)
+        for quarter in range(4):
+            place = (quarter % 2) * 1024 + (2 * block + quarter // 2) * 64
+            weight_src[pl.ds(pl.multiple_of(place, 64), 64), :] = share_w[
+                64 * quarter : 64 * quarter + 64
+            ]
+    send(
+        weight_src.at[rows_of(1 - core, 1024)],
+        weight_pair,
+        seq_send.at[4],
+        seq_recv.at[4],
+        {"seq": 2 * chip + 1 - core},
+    )
     for b in range(4):
         grad_out, grad_gate = gated_back(
             outs_s[b], block_of(gate_ref, b), stack_heads(grad_normed[SPAN * b : SPAN * b + SPAN])
@@ -650,70 +673,21 @@
             ].astype(BF16)
 
     def send_grads(offset, carry):
-        to = (me + offset) % N_SEQ
+        to = lax.rem(chip + offset, CHIPS)
         send(
-            grad_src.at[rows_of(to // 2, 32)],
+            grad_src.at[rows_of(to, 32)],
             grad_pieces.at[rows_of(offset - 1, 32)],
             seq_send.at[2],
             seq_recv.at[2],
-            {"seq": to},
+            {"seq": 2 * to + core},
         )
         return carry
 
-    lax.fori_loop(1, N_SEQ, send_grads, 0)
-    grad_pieces[992:1024, :] = grad_src[rows_of(chip, 32), :]
+    lax.fori_loop(1, CHIPS, send_grads, 0)
+    grad_pieces[480:512, :] = grad_src[rows_of(chip, 32), :]
 
     sums_prepare(3)
     sums_pump(1)
-
-    for index, (slot_ref, block) in enumerate(cot_slots()):
-        share_w = dot(slot_ref[...], normed_s[...], "tn").astype(BF16)
-        for quarter in range(4):
-            place = (quarter % 2) * 1024 + (2 * block + quarter // 2) * 64
-            weight_src[pl.ds(pl.multiple_of(place, 64), 64), :] = share_w[
-                64 * quarter : 64 * quarter + 64
-            ]
-        if index % 2 == 1:
-            sums_pump(1)
-    send(
-        weight_src.at[rows_of(1 - core, 1024)],
-        weight_pair,
-        seq_send.at[4],
-        seq_recv.at[4],
-        {"seq": 2 * chip + 1 - core},
-    )
-
-    sums_prepare(4)
-    _, col = iotas((1, 128))
-    row, _ = iotas((256, 1))
-    target = 2 * ((chip + 1 + (row >> 4)) % CHIPS) + core
-    for part in range(8):
-        owner = jnp.full((1, 128), -1, jnp.int32)
-        for index in range(4):
-            device = (me + 31 - (4 * part + index)) % N_SEQ
-            for slot in range(2):
-                owner = jnp.where((col >> 4) == 2 * index + slot, owner_of(device, slot), owner)
-        here = (owner == target) & ((row & 15) == (col & 15))
-        gather_s[:, 128 * part : 128 * part + 128] = jnp.where(here, 1.0, 0.0).astype(BF16)
-    sums_pump(1)
-
-    await_bytes(grad_pieces.at[pl.ds(0, 992)], seq_recv.at[2])
-
-    owned_src[...] = dot(gather_s[...], grad_pieces[...]).astype(BF16)
-
-    def send_owned(offset, carry):
-        send(
-            owned_src.at[rows_of(offset - 1, 16)],
-            owned.at[rows_of(offset - 1, 16)],
-            seq_send.at[3],
-            seq_recv.at[3],
-            {"seq": 2 * ((chip + offset) % CHIPS) + core},
-        )
-        return carry
-
-    lax.fori_loop(1, CHIPS, send_owned, 0)
-    sums_pump(1)
-    owned[240:256, :] = owned_src[240:256, :]
 
     await_bytes(weight_pair, seq_recv.at[4])
     for part in range(4):
@@ -724,7 +698,7 @@
         ).astype(BF16)
 
     def send_weight(offset, carry):
-        to = (chip + offset) % CHIPS
+        to = lax.rem(chip + offset, CHIPS)
         send(
             weight_sum.at[rows_of(to, 64)],
             weight_in.at[rows_of(offset - 1, 64)],
@@ -734,7 +708,40 @@
         )
         return carry
 
-    lax.fori_loop(1, CHIPS, send_weight, 0)
+    lax.fori_loop(1, 12, send_weight, 0)
+    sums_pump(4)
+    sums_prepare(4)
+    _, col = iotas((1, 128))
+    row, _ = iotas((512, 1))
+    target = (me + 1 + (row >> 4)) % N_SEQ
+    for part in range(4):
+        owner = jnp.full((1, 128), -1, jnp.int32)
+        for index in range(4):
+            device = 2 * lax.rem(chip + 31 - (4 * part + index), CHIPS) + core
+            for slot in range(2):
+                owner = jnp.where((col >> 4) == 2 * index + slot, owner_of(device, slot), owner)
+        here = (owner == target) & ((row & 15) == (col & 15))
+        gather_s[:, 128 * part : 128 * part + 128] = jnp.where(here, 1.0, 0.0).astype(BF16)
+
+    await_bytes(grad_pieces.at[pl.ds(0, 480)], seq_recv.at[2])
+
+    owned_src[...] = dot(gather_s[...], grad_pieces[...]).astype(BF16)
+
+    def send_owned(offset, carry):
+        send(
+            owned_src.at[rows_of(offset - 1, 16)],
+            owned.at[rows_of(offset - 1, 16)],
+            seq_send.at[3],
+            seq_recv.at[3],
+            {"seq": lax.rem(me + offset, N_SEQ)},
+        )
+        return carry
+
+    lax.fori_loop(1, N_SEQ, send_owned, 0)
+    sums_pump(2)
+    owned[496:512, :] = owned_src[496:512, :]
+
+    lax.fori_loop(12, CHIPS, send_weight, 0)
 
     grad_cums, grad_rates, grad_rows = [None] * 4, [None] * 4, [None] * 4
 
@@ -768,12 +775,13 @@
             sums_pump(1)
 
     share_s[0] = share(0)
-    await_bytes(owned.at[pl.ds(0, 240)], seq_recv.at[3])
+    await_bytes(owned.at[pl.ds(0, 496)], seq_recv.at[3])
     for piece in range(CHIPS):
-        place = (chip - piece + 15) % CHIPS
-        grad_state_s[0, 16 * (piece % 8) : 16 * (piece % 8) + 16, 128 * (piece // 8) : 128 * (piece // 8) + 128] = (
-            owned[rows_of(place, 16), :].astype(F32)
-        )
+        low, lane = 16 * (piece % 8), 128 * (piece // 8)
+        one, two = [lax.rem(me + 63 - (2 * piece + side), N_SEQ) for side in range(2)]
+        grad_state_s[0, low : low + 16, lane : lane + 128] = owned[rows_of(one, 16), :].astype(
+            F32
+        ) + owned[rows_of(two, 16), :].astype(F32)
     grad_state = grad_state_s[0]
     grad_update = dot(scores_s[0], grad_out_s[0], "tn")
     grad_update += cols[0][4] * stack_heads(dot(keys[0], grad_state))
@@ -793,8 +801,8 @@
     await_bytes(sums.at[pl.ds(0, 7)], sum_send.at[0])
     await_bytes(pieces.at[pl.ds(0, 496)], seq_send.at[0])
     await_bytes(chosen.at[pl.ds(0, 480)], seq_send.at[1])
-    await_bytes(grad_pieces.at[pl.ds(0, 992)], seq_send.at[2])
-    await_bytes(owned.at[pl.ds(0, 240)], seq_send.at[3])
+    await_bytes(grad_pieces.at[pl.ds(0, 480)], seq_send.at[2])
+    await_bytes(owned.at[pl.ds(0, 496)], seq_send.at[3])
     await_bytes(weight_pair, seq_send.at[4])
     await_bytes(weight_in.at[pl.ds(0, 15 * 64)], seq_send.at[5])
 
@@ -815,9 +823,9 @@
     pltpu.VMEM((512, 128), BF16),
     pltpu.VMEM((2, 128, 256), F32),
     pltpu.VMEM((512, 128), BF16),
-    pltpu.VMEM((1024, 128), BF16),
-    pltpu.VMEM((256, 128), BF16),
-    pltpu.VMEM((256, 128), BF16),
+    pltpu.VMEM((512, 128), BF16),
+    pltpu.VMEM((512, 128), BF16),
+    pltpu.VMEM((512, 128), BF16),
     pltpu.VMEM((8, 256, 256), BF16),
     pltpu.VMEM((8, 256, 256), BF16),
     pltpu.VMEM((2048, 256), BF16),
@@ -838,8 +846,9 @@
     pltpu.VMEM((3, 128, 128), F32),
     pltpu.VMEM((256, 256), BF16),
     pltpu.VMEM((8, 256, 256), F32),
+    pltpu.VMEM((8, 256, 256), BF16),
     pltpu.VMEM((512, 512), BF16),
-    pltpu.VMEM((256, 1024), BF16),
+    pltpu.VMEM((512, 512), BF16),
     pltpu.SemaphoreType.DMA((8,)),
     pltpu.SemaphoreType.DMA((1,)),
     pltpu.SemaphoreType.DMA((32,)),

time: 51.1 us -> 49.6 us (0.971)
  Pallas kernels: 50.4 us -> 48.8 us
    pallas_call x1, Pallas kernels: 48.2 us -> 46.7 us  [per_device(): pl.pallas_call(layer_kernel, out_shape=RESULTS, in_specs=[whole] * 8 + [s...]
where the time goes in v5:
time: 49.6 us; the launch traced here: 49.5 us
  Pallas kernels  48.8 us (98%)
  between operations  0.64 us (1%)
    pallas_call x1, Pallas kernels, per_device(): pl.pallas_call(layer_kernel, out_shape=RESULTS, in_specs=[whole] * 8 + [s...  46.7 us
    pallas_call x1, Pallas kernels, per_device(): pl.pallas_call(finish_kernel, out_shape=RESULTS, in_specs=[vmem] * 8, out...  2.17 us

profile of v5, /device:TPU:1, one launch (start us, length us, event | category | flops | bytes accessed | tf_op | source)
XLA Modules:
  0.0 49.5 jit_solution(11723135815424910598)
XLA Ops:
  0.6 46.7 %shard_map.161 = (bf16[256,256]{1,0:T(8,128)(2,1)}, f32[256,128]{1,0:T(8,128)}, f32[256,128]{1,0:T(8,128)}, f32[256,256]{1,0:T(8,128)}, f32[256,256]{1,0:T(8,128...) custom-call(bf16[256,128]{1,0:T(8,128)(2,1)} %query_hbm.1, bf16[256,128]{1,0:T(8,128)(2,1)} %key_hbm.1, ...), custom_call_target="tpu_custom_call" | custom-call | tf_op jit(solution)/shard_map/pallas_call | solution.py:886
  47.3 2.2 %shard_map.162 = (bf16[256,256]{1,0:T(8,128)(2,1)}, f32[256,128]{1,0:T(8,128)}, f32[256,128]{1,0:T(8,128)}, f32[256,256]{1,0:T(8,128)}, f32[256,256]{1,0:T(8,128...) custom-call(bf16[256,256]{1,0:T(8,128)(2,1)} %get-tuple-element.16.refs_0_, ...), custom_call_target="tpu_custom_call" | custom-call | tf_op jit(solution)/shard_map/pallas_call | solution.py:899

commit v6 on v5

--- a/solution.py
+++ b/solution.py
@@ -177,23 +177,28 @@
     return inv * (weighted - out * (inv * inv * along)), grad_gate
 
 
+def score_grads(query, key, tables, update, grad_out):
+    within, _, query_key = tables
+    grad_scores = dot3(grad_out, update, "nt")
+    masked = grad_scores * within
+    return grad_scores * query_key, fold(dot(masked, twice(key))), dot(masked, twice(query), "tn")
+
+
 def block_grads(
-    query, key, value, cols, growth_last, tables, step, update, grad_out, grad_state, state_in
+    key, value, cols, growth_last, tables, step, update, grad_out, grad_state, state_in, scored
 ):
     _, _, rate, growth, remain = cols
-    within, system, query_key = tables
+    within, system, _ = tables
+    scored_spread, grad_query, scored_key = scored
     row, col = iotas()
-    key2, query2 = twice(key), twice(query)
-    grad_scores = dot3(grad_out, update, "nt")
+    key2 = twice(key)
     grad_system = -dot(step, update, "nt")
-    masked = grad_scores * within
     strict = jnp.where(row > col, grad_system * within, 0.0) * rate
     pulled = grad_system * system
-    spread = grad_scores * query_key + pulled
-    grad_query = fold(dot(masked, key2))
+    spread = scored_spread + pulled
     state_key = dot(diagonal_heads(update), grad_state, "nt")
     grad_key = fold(
-        dot(masked, query2, "tn") + dot(strict, key2) + dot(strict, key2, "tn") + remain * state_key
+        scored_key + dot(strict, key2) + dot(strict, key2, "tn") + remain * state_key
     )
     tail = remain * jnp.sum(key2 * state_key, axis=-1, keepdims=True)
     grad_cum = jnp.sum(spread, axis=-1, keepdims=True) - tail
@@ -708,7 +713,7 @@
         )
         return carry
 
-    lax.fori_loop(1, 12, send_weight, 0)
+    lax.fori_loop(1, CHIPS, send_weight, 0)
     sums_pump(4)
     sums_prepare(4)
     _, col = iotas((1, 128))
@@ -741,24 +746,28 @@
     sums_pump(2)
     owned[496:512, :] = owned_src[496:512, :]
 
-    lax.fori_loop(12, CHIPS, send_weight, 0)
 
     grad_cums, grad_rates, grad_rows = [None] * 4, [None] * 4, [None] * 4
 
-    def finish_block(b, grad_state, state_in):
-        tables = (within_s[b], system_s[b], scores_s[b])
+    def tables_found(b):
+        return within_s[b], system_s[b], scores_s[b]
+
+    def scored_of(b):
+        return score_grads(queries[b], keys[b], tables_found(b), update_s[b], grad_out_s[b])
+
+    def finish_block(b, grad_state, state_in, scored):
         found = block_grads(
-            queries[b],
             keys[b],
             block_of(value_ref, b),
             cols[b],
             last_growth(rows, b),
-            tables,
+            tables_found(b),
             step_s[b],
             update_s[b],
             grad_out_s[b],
             grad_state,
             state_in,
+            scored,
         )
         for raw_ref, out_ref, grad, scale in (
             (query_ref, grad_query_ref, found[0], SCALE),
@@ -770,11 +779,19 @@
         grad_rates[b], grad_cums[b], grad_rows[b] = found[3:]
 
     for b in (1, 2, 3):
-        finish_block(b, grad_state_s[b], (state_s[b - 1], key_state_s[b - 1], query_state_s[b - 1]))
+        state_in = (state_s[b - 1], key_state_s[b - 1], query_state_s[b - 1])
+        finish_block(b, grad_state_s[b], state_in, scored_of(b))
         if b < 3:
             sums_pump(1)
 
     share_s[0] = share(0)
+    scored = scored_of(0)
+    grad_update = dot(scores_s[0], grad_out_s[0], "tn")
+    await_bytes(weight_in.at[pl.ds(0, 15 * 64)], seq_recv.at[5])
+    total = weight_sum[rows_of(chip, 64), :].astype(F32)
+    for slot in range(15):
+        total += weight_in[64 * slot : 64 * slot + 64, :].astype(F32)
+    grad_weight_ref[...] = total
     await_bytes(owned.at[pl.ds(0, 496)], seq_recv.at[3])
     for piece in range(CHIPS):
         low, lane = 16 * (piece % 8), 128 * (piece // 8)
@@ -783,17 +800,11 @@
             F32
         ) + owned[rows_of(two, 16), :].astype(F32)
     grad_state = grad_state_s[0]
-    grad_update = dot(scores_s[0], grad_out_s[0], "tn")
     grad_update += cols[0][4] * stack_heads(dot(keys[0], grad_state))
     step_s[0] = dot(inverse_s[0], grad_update, "tn")
-    finish_block(0, grad_state, None)
+    finish_block(0, grad_state, None, scored)
     grad_rate_ref[...], grad_decay_ref[...] = decay_grads(grad_cums, grad_rates, grad_rows)
 
-    await_bytes(weight_in.at[pl.ds(0, 15 * 64)], seq_recv.at[5])
-    total = weight_sum[rows_of(chip, 64), :].astype(F32)
-    for slot in range(15):
-        total += weight_in[64 * slot : 64 * slot + 64, :].astype(F32)
-    grad_weight_ref[...] = total
     sums_pump(4)
     layer_ref[...] = (share_s[0] + sums[6].astype(F32) + sums[7].astype(F32)).astype(BF16)
 

time: 49.6 us -> 49 us (0.988)
  Pallas kernels: 48.8 us -> 48.2 us
    pallas_call x1, Pallas kernels: 46.7 us -> 46.1 us  [per_device(): pl.pallas_call(layer_kernel, out_shape=RESULTS, in_specs=[whole] * 8 + [s...]
where the time goes in v6:
time: 49 us; the launch traced here: 48.9 us
  Pallas kernels  48.2 us (98%)
  between operations  0.64 us (1%)
    pallas_call x1, Pallas kernels, per_device(): pl.pallas_call(layer_kernel, out_shape=RESULTS, in_specs=[whole] * 8 + [s...  46.1 us
    pallas_call x1, Pallas kernels, per_device(): pl.pallas_call(finish_kernel, out_shape=RESULTS, in_specs=[vmem] * 8, out...  2.17 us

profile of v6, /device:TPU:1, one launch (start us, length us, event | category | flops | bytes accessed | tf_op | source)
XLA Modules:
  0.0 48.9 jit_solution(5309290183814401530)
XLA Ops:
  0.6 46.1 %shard_map.161 = (bf16[256,256]{1,0:T(8,128)(2,1)}, f32[256,128]{1,0:T(8,128)}, f32[256,128]{1,0:T(8,128)}, f32[256,256]{1,0:T(8,128)}, f32[256,256]{1,0:T(8,128...) custom-call(bf16[256,128]{1,0:T(8,128)(2,1)} %query_hbm.1, bf16[256,128]{1,0:T(8,128)(2,1)} %key_hbm.1, ...), custom_call_target="tpu_custom_call" | custom-call | tf_op jit(solution)/shard_map/pallas_call | solution.py:897
  46.7 2.2 %shard_map.162 = (bf16[256,256]{1,0:T(8,128)(2,1)}, f32[256,128]{1,0:T(8,128)}, f32[256,128]{1,0:T(8,128)}, f32[256,256]{1,0:T(8,128)}, f32[256,256]{1,0:T(8,128...) custom-call(bf16[256,256]{1,0:T(8,128)(2,1)} %get-tuple-element.16.refs_0_, ...), custom_call_target="tpu_custom_call" | custom-call | tf_op jit(solution)/shard_map/pallas_call | solution.py:910

commit v7 on v6

--- a/solution.py
+++ b/solution.py
@@ -614,6 +614,7 @@
 
     loads[7].wait()
     sums_begin()
+    sums_prepare(3)
     for index, (slot_ref, _) in enumerate(cot_slots()):
         if index in (5, 6):
             turn(index, slot_ref)
@@ -691,7 +692,6 @@
     lax.fori_loop(1, CHIPS, send_grads, 0)
     grad_pieces[480:512, :] = grad_src[rows_of(chip, 32), :]
 
-    sums_prepare(3)
     sums_pump(1)
 
     await_bytes(weight_pair, seq_recv.at[4])
@@ -714,8 +714,8 @@
         return carry
 
     lax.fori_loop(1, CHIPS, send_weight, 0)
+    sums_prepare(4)
     sums_pump(4)
-    sums_prepare(4)
     _, col = iotas((1, 128))
     row, _ = iotas((512, 1))
     target = (me + 1 + (row >> 4)) % N_SEQ
@@ -727,6 +727,7 @@
                 owner = jnp.where((col >> 4) == 2 * index + slot, owner_of(device, slot), owner)
         here = (owner == target) & ((row & 15) == (col & 15))
         gather_s[:, 128 * part : 128 * part + 128] = jnp.where(here, 1.0, 0.0).astype(BF16)
+    sums_pump(1)
 
     await_bytes(grad_pieces.at[pl.ds(0, 480)], seq_recv.at[2])
 
@@ -743,7 +744,7 @@
         return carry
 
     lax.fori_loop(1, N_SEQ, send_owned, 0)
-    sums_pump(2)
+    sums_pump(1)
     owned[496:512, :] = owned_src[496:512, :]
 
 
@@ -871,8 +872,17 @@
 
 
 def finish_kernel(*refs):
-    for index in range(8):
-        refs[8 + index][...] = refs[index][...]
+    given, results, held = refs[:8], refs[8:16], refs[16:24]
+    sems = refs[24]
+    reads = [pltpu.make_async_copy(given[i], held[i], sems.at[i]) for i in range(8)]
+    writes = [pltpu.make_async_copy(held[i], results[i], sems.at[8 + i]) for i in range(8)]
+    for read in reads:
+        read.start()
+    for read, write in zip(reads, writes):
+        read.wait()
+        write.start()
+    for write in writes:
+        write.wait()
 
 
 RESULTS = [
@@ -910,8 +920,11 @@
     return pl.pallas_call(
         finish_kernel,
         out_shape=RESULTS,
-        in_specs=[vmem] * 8,
-        out_specs=[vmem] * 8,
+        in_specs=[whole] * 8,
+        out_specs=[whole] * 8,
+        scratch_shapes=[pltpu.VMEM(one.shape, one.dtype) for one in RESULTS]
+        + [pltpu.SemaphoreType.DMA((16,))],
+        compiler_params=pltpu.CompilerParams(vmem_limit_bytes=56 * 1024 * 1024),
     )(*results)
 
 

time: 49 us -> 49 us (level)
  no operation moved by 1% of the time
where the time goes in v7:
time: 49 us; the launch traced here: 48.8 us
  Pallas kernels  48.2 us (98%)
  between operations  0.64 us (1%)
    pallas_call x1, Pallas kernels, per_device(): pl.pallas_call(layer_kernel, out_shape=RESULTS, in_specs=[whole] * 8 + [s...  46.1 us
    pallas_call x1, Pallas kernels, per_device(): pl.pallas_call(finish_kernel, out_shape=RESULTS, in_specs=[whole] * 8, ou...  2.1 us

profile of v7, /device:TPU:1, one launch (start us, length us, event | category | flops | bytes accessed | tf_op | source)
XLA Modules:
  0.0 48.8 jit_solution(11295580152294667862)
XLA Ops:
  0.6 46.1 %shard_map.161 = (bf16[256,256]{1,0:T(8,128)(2,1)}, f32[256,128]{1,0:T(8,128)}, f32[256,128]{1,0:T(8,128)}, f32[256,256]{1,0:T(8,128)}, f32[256,256]{1,0:T(8,128...) custom-call(bf16[256,128]{1,0:T(8,128)(2,1)} %query_hbm.1, bf16[256,128]{1,0:T(8,128)(2,1)} %key_hbm.1, ...), custom_call_target="tpu_custom_call" | custom-call | tf_op jit(solution)/shard_map/pallas_call | solution.py:907
  46.7 2.1 %shard_map.162 = (bf16[256,256]{1,0:T(8,128)(2,1)}, f32[256,128]{1,0:T(8,128)}, f32[256,128]{1,0:T(8,128)}, f32[256,256]{1,0:T(8,128)}, f32[256,256]{1,0:T(8,128...) custom-call(bf16[256,256]{1,0:T(8,128)(2,1)} %get-tuple-element.16.refs_0_, ...), custom_call_target="tpu_custom_call" | custom-call | tf_op jit(solution)/shard_map/pallas_call | solution.py:920
